TPU v7x, 32 devices: a whole 2x2x4 slice. The times are simulated.
32 devices in a mesh: groups: 2 (over x), centers: 16 (over z, y, core).
Axes of the slice: x: 2, y: 2, z: 4, core: 2. Of those that a mesh axis runs over, the one named last changes fastest.
Arguments:
- center_feats: bfloat16 [32768, 1024], P(('groups', 'centers')), parts along dimension 0, may hold values from -8 to 8
- coeffs: bfloat16 [32768, 1000], P(('groups', 'centers')), parts along dimension 0, may hold values from -0.119628906 to 0.119628906
- labels: bfloat16 [256, 1000], P(('groups', 'centers')), parts along dimension 0, may hold values from -6 to 6
- running: float32 [256, 1000], P(('groups', 'centers')), parts along dimension 0, may hold values from -6 to 6
- batch_index: int32 [256], P(('groups', 'centers')), parts along dimension 0, may hold values from 0 to 16383, as said below
- landmark_index: int32 [4096], P(('groups', 'centers')), parts along dimension 0, may hold values from 0 to 16383, as said below
Outputs:
- new_running: float32 [256, 1000], P(('groups', 'centers')), parts along dimension 0
- projection: float32 [4096, 1000], P(('groups', 'centers')), parts along dimension 0
There are 2 independent parts, one for each index of `groups`. A program takes and returns all parts, laid end to end along the dimension named above; each array names one. Nothing has to cross between parts.
Inputs may be any that keep to these rules, and one draw needn't show every extreme that they name: The entries of batch_index in rows j * 8 to (j + 1) * 8 - 1 are distinct and lie in j * 1024 to (j + 1) * 1024 - 1. The entries of landmark_index in rows j * 128 to (j + 1) * 128 - 1 are distinct and lie in j * 1024 to (j + 1) * 1024 - 1.
All inputs are finite; a program needn't handle non-finite values.
Results may differ from a plain program's by a relative error of at most 0.002.
Values may be sent and summed in bfloat16 or wider, within the bound.
No kernel may reach another device: no remote copies, remote signals or barrier semaphores. Data moves between devices by JAX's collectives and lax.ppermute only.
A program may use at most 64 MiB of HBM per device.

v0:
```python
import jax
import jax.numpy as jnp
from jax import lax
from jax.sharding import PartitionSpec as P

D = 1024


def squared_norms(feats):
    return jnp.sum(feats.astype(jnp.float32) ** 2, axis=-1)


def kernel_from(row_feats, row_norms, col_feats, col_norms):
    cross = jnp.dot(row_feats, col_feats.T, preferred_element_type=jnp.float32)
    dist = row_norms[:, None] + col_norms[None, :] - 2.0 * cross
    return jnp.exp(-dist / D).astype(jnp.bfloat16)


def per_device(center_feats, coeffs, labels, running, batch_index, landmark_index):
    slab_rows = center_feats.shape[0]
    offset_rows = lax.axis_index("centers") * slab_rows
    own_feats = jnp.take(center_feats, batch_index - offset_rows, axis=0)
    land_local = landmark_index - offset_rows
    batch_feats = lax.all_gather(own_feats, "centers", axis=0, tiled=True)
    center_norms = squared_norms(center_feats)
    batch_norms = squared_norms(batch_feats)
    tile = kernel_from(batch_feats, batch_norms, center_feats, center_norms)
    pred = lax.psum_scatter(
        jnp.dot(tile, coeffs, preferred_element_type=jnp.float32),
        "centers",
        scatter_dimension=0,
        tiled=True,
    )
    new_running = running + pred
    resid_own = (new_running - labels.astype(jnp.float32)).astype(jnp.bfloat16)
    resid_all = lax.all_gather(resid_own, "centers", axis=0, tiled=True)
    land_feats = jnp.take(center_feats, land_local, axis=0)
    land_norms = jnp.take(center_norms, land_local, axis=0)
    projection = jnp.dot(
        kernel_from(land_feats, land_norms, batch_feats, batch_norms),
        resid_all,
        preferred_element_type=jnp.float32,
    )
    return (new_running, projection)


def solution(mesh):
    placed = (
        P(("groups", "centers"), None),
        P(("groups", "centers"), None),
        P(("groups", "centers"), None),
        P(("groups", "centers"), None),
        P(("groups", "centers")),
        P(("groups", "centers")),
    )
    return jax.shard_map(
        per_device,
        mesh=mesh,
        in_specs=placed,
        out_specs=(P(("groups", "centers"), None), P(("groups", "centers"), None)),
        check_vma=False,
    )
```

profile of v0, /device:TPU:0, one launch (start us, length us, event | category | flops | bytes accessed | tf_op | source)
XLA Modules:
  0.0 122.9 jit_solution(11632106637541940374)
XLA Ops:
  7.2 0.0 copy-start
  7.2 0.0 copy-start.3
  7.2 0.0 reduce-scatter.2.cloned.1.call-start
  7.2 2.2 %multiply_reduce_fusion = f32[1024]{0:T(1024)S(1)} fusion(bf16[1024,1024]{1,0:T(8,128)(2,1)} %param.6), kind=kLoop, calls=%fused_computation.3 | loop fusion | flops 3144704 | bytes 2101248 | tf_op jit(solution)/shard_map/reduce_sum | solution.py:10
  9.4 0.0 copy-done.3
  9.5 2.4 %gather_fusion = bf16[8,1024]{1,0:T(8,128)(2,1)S(1)} fusion(bf16[1024,1024]{1,0:T(8,128)(2,1)} %param.6, s32[1024]{0:T(1024)S(1)} %pad_clamp_fusion.1), kind=kCustom, calls=%fused_computation | custom fusion | bytes 32800 | tf_op jit(solution)/shard_map/jit(_take)/gather | solution.py:22
  11.9 0.1 broadcast_select_fusion
  12.0 23.8 %all_gather.6 = bf16[128,1024]{1,0:T(8,128)(2,1)S(1)} all-gather(bf16[8,1024]{1,0:T(8,128)(2,1)S(1)} %broadcast_select_fusion), channel_id=1, replica_groups=mesh['groups'=2,'centers'=16] {'centers'}, dimensions={0}, use_global_device_ids=true | all-gather | bytes 278528 | tf_op jit(solution)/shard_map/all_gather | solution.py:24
  35.8 0.1 multiply_reduce_fusion.1
  35.9 0.0 copy-done
  35.9 0.0 copy-start.4
  35.9 3.9 %fusion.5 = f32[128,1000]{1,0:T(8,128)} fusion(bf16[1024,1000]{0,1:T(8,128)(2,1)S(1)} %copy-done, bf16[128,1024]{1,0:T(8,128)(2,1)S(1)} %all_gather.6, bf16[1024,1024]{1,0:T(8,128)(2,1)} %param.6, f32[1024]{0:T(1024)S(1)} %multiply_reduce_fusion, f32[128]{0:T(128)S(1)} %multiply_reduce_fusion.1), kind=kOutput, calls=%fused_computation.10 | convolution fusion | flops 531365888 | bytes 4923904 | tf_op jit(solution)/shard_map/dot_general | solution.py:29
  39.8 0.0 copy-start.1
  39.8 0.0 copy-start.2
  39.8 0.0 reduce-scatter.2.cloned.1.call-update
  39.9 0.0 copy-done.4
  39.9 1.0 gather_fusion.1
  40.9 2.9 %gather_fusion.2 = bf16[128,1024]{1,0:T(8,128)(2,1)S(1)} fusion(bf16[1024,1024]{1,0:T(8,128)(2,1)} %param.6, s32[1024]{0:T(1024)S(1)} %pad_clamp_fusion), kind=kCustom, calls=%fused_computation.2 | custom fusion | bytes 524800 | tf_op jit(solution)/shard_map/jit(_take)/gather | solution.py:37
  43.8 49.3 %reduce-scatter.2.cloned.1.call-done = f32[8,1000]{1,0:T(8,128)} async-done(((f32[128,1000]{1,0:T(8,128)}), f32[8,1000]{1,0:T(8,128)}) %reduce-scatter.2.cloned.1.call-update) | async-done | bytes 32016 | tf_op jit(solution)/shard_map/reduce_scatter | solution.py:28
  93.1 0.0 copy-done.1
  93.1 0.0 copy-done.2
  93.1 1.4 %subtract_convert_fusion = (bf16[8,1000]{1,0:T(8,128)(2,1)S(1)}, f32[8,1000]{1,0:T(8,128)}) fusion(bf16[8,1000]{1,0:T(8,128)(2,1)S(1)} %copy-done.2, f32[8,1000]{1,0:T(8,128)S(1)} %copy-done.1, f32[8,1000]{1,0:T(8,128)} %reduce-scatter.2.cloned.1.call-done), kind=kLoop, calls=%fused_computation.28 | loop fusion | flops 32000 | bytes 128000 | tf_op jit(solution)/shard_map/convert_element_type | solution.py:35
  94.5 20.1 %all_gather.7 = bf16[128,1000]{1,0:T(8,128)(2,1)S(1)} all-gather(bf16[8,1000]{1,0:T(8,128)(2,1)S(1)} %get-tuple-element.4), channel_id=1, replica_groups=mesh['groups'=2,'centers'=16] {'centers'}, dimensions={0}, use_global_device_ids=true | all-gather | bytes 272000 | tf_op jit(solution)/shard_map/all_gather | solution.py:36
  114.6 1.5 %fusion.11 = f32[128,1000]{0,1:T(8,128)} fusion(bf16[128,1000]{1,0:T(8,128)(2,1)S(1)} %all_gather.7, bf16[128,1024]{1,0:T(8,128)(2,1)S(1)} %all_gather.6, bf16[128,1024]{1,0:T(8,128)(2,1)S(1)} %gather_fusion.2, pred[128]{0:T(512)(128)(4,1)S(1)} %get-tuple-element.2, f32[128]{0:T(128)S(1)} %multiply_reduce_fusion.1, f32[128]{0:T(128)S(1)} %broadcast_select_fusion.1), kind=kOutput, calls=%fused_computation.17 | convolution fusion | flops 66551808 | bytes 1293440 | tf_op jit(solution)/shard_map/dot_general | solution.py:39
  (5 shorter events, 0.0 us)
Async XLA Ops:
  7.2 28.8 %copy-start = (bf16[1024,1000]{0,1:T(8,128)(2,1)S(1)}, bf16[1024,1000]{0,1:T(8,128)(2,1)}, u32[]{:S(2)}) copy-start(bf16[1024,1000]{0,1:T(8,128)(2,1)} %param.7) | copy-start | bytes 6144004
  7.2 2.3 %copy-start.3 = (s32[8]{0:T(128)S(1)}, s32[8]{0:T(128)}, u32[]{:S(2)}) copy-start(s32[8]{0:T(128)} %param.10) | copy-start | bytes 100
  7.2 85.9 %reduce-scatter.2.cloned.1.call-start = ((), (), s32[]{:S(2)}) async-start(), calls=%async_computation.1 | async-start | bytes 557056 | tf_op jit(solution)/shard_map/reduce_scatter | solution.py:28
  35.9 3.9 %copy-start.4 = (s32[128]{0:T(128)S(1)}, s32[128]{0:T(128)}, u32[]{:S(2)}) copy-start(s32[128]{0:T(128)} %param.11) | copy-start | bytes 1540
  39.8 53.2 %copy-start.1 = (f32[8,1000]{1,0:T(8,128)S(1)}, f32[8,1000]{1,0:T(8,128)}, u32[]{:S(2)}) copy-start(f32[8,1000]{1,0:T(8,128)} %param.9) | copy-start | bytes 96004
  39.8 53.2 %copy-start.2 = (bf16[8,1000]{1,0:T(8,128)(2,1)S(1)}, bf16[8,1000]{1,0:T(8,128)(2,1)}, u32[]{:S(2)}) copy-start(bf16[8,1000]{1,0:T(8,128)(2,1)} %param.8) | copy-start | bytes 48004
Sparse Core Ops, SparseCore 0:
  40.0 53.0 reduce-scatter.1
where the time goes:
time: 123 us
  waiting for transfers between devices  49.3 us (40%)
  blocking collectives  43.9 us (36%)
  between operations  14.1 us (11%)
  local copies, waits for them, and re-layouts  6.35 us (5%)
  matrix products  5.35 us (4%)
  other arithmetic  3.83 us (3%)
    reduce_scatter x1, waiting for transfers between devices, per_device(): lax.psum_scatter(jnp.dot(tile, coeffs, preferred_element_type=jnp.float32...  49.3 us
    all_gather x1, blocking collectives, per_device(): batch_feats = lax.all_gather(own_feats, 'centers', axis=0, tiled=True)  23.8 us
    all_gather x1, blocking collectives, per_device(): resid_all = lax.all_gather(resid_own, 'centers', axis=0, tiled=True)  20.1 us
    dot_general x1, matrix products, per_device(): jnp.dot(tile, coeffs, preferred_element_type=jnp.float32)  3.89 us
    gather x1, local copies, waits for them, and re-layouts, per_device(): land_feats = jnp.take(center_feats, land_local, axis=0)  2.91 us
  transfers between devices with their start and end apart: 1, of which 1 were waited for; matrix products, arithmetic and copies ran while one was open for 3% of the time, Pallas kernels for 0%

commit v1 on v0

v1 whole, which is shorter than its diff:
```python
import functools

import jax
import jax.numpy as jnp
from jax import lax
from jax.experimental import pallas as pl
from jax.experimental.pallas import tpu as pltpu
from jax.sharding import PartitionSpec as P

SCALE = 1024.0
VMEM_LIMIT = 48 * 1024 * 1024


def gather_kernel(index_ref, feats_ref, out_ref, blocks, rows_out, sems):
    picks = index_ref.shape[0]
    slab = feats_ref.shape[0]
    copies = []
    for i in range(picks):
        row = lax.rem(index_ref[i], slab)
        start = pl.multiple_of((row // 16) * 16, 16)
        copy = pltpu.make_async_copy(
            feats_ref.at[pl.ds(start, 16), :], blocks.at[i], sems.at[i]
        )
        copy.start()
        copies.append(copy)
    for i in range(picks):
        copies[i].wait()
        inside = lax.rem(index_ref[i], 16)
        block = blocks[i].astype(jnp.float32)
        here = lax.broadcasted_iota(jnp.int32, block.shape, 0) == inside
        rows_out[i : i + 1, :] = jnp.sum(
            jnp.where(here, block, 0.0), axis=0, keepdims=True
        )
    rows = rows_out[...].astype(out_ref.dtype)
    for chip in range(out_ref.shape[0]):
        out_ref[chip] = rows


def gather_rows(center_feats, batch_index, chips):
    picks, width = batch_index.shape[0], center_feats.shape[1]
    return pl.pallas_call(
        gather_kernel,
        out_shape=jax.ShapeDtypeStruct((chips, picks, width), center_feats.dtype),
        in_specs=[
            pl.BlockSpec(memory_space=pltpu.SMEM),
            pl.BlockSpec(memory_space=pltpu.HBM),
        ],
        out_specs=pl.BlockSpec(memory_space=pltpu.VMEM),
        scratch_shapes=[
            pltpu.VMEM((picks, 16, width), center_feats.dtype),
            pltpu.VMEM((picks, width), jnp.float32),
            pltpu.SemaphoreType.DMA((picks,)),
        ],
        compiler_params=pltpu.CompilerParams(vmem_limit_bytes=VMEM_LIMIT),
    )(batch_index, center_feats)


def nt(a, b):
    return lax.dot_general(
        a, b, (((1,), (1,)), ((), ())), preferred_element_type=jnp.float32
    )


def tile_kernel(mine_ref, other_ref, feats_ref, coeffs_ref, land_ref,
                pred_mine_ref, pred_other_ref, land_tile_ref):
    slab = feats_ref.shape[0]
    half = mine_ref.shape[0]
    batch = jnp.concatenate([mine_ref[...], other_ref[...]], axis=0)
    feats = feats_ref[...]
    wide = feats.astype(jnp.float32)
    center_norms = jnp.sum(wide * wide, axis=1, keepdims=True)
    batch_wide = batch.astype(jnp.float32)
    batch_norms = jnp.sum(batch_wide * batch_wide, axis=1, keepdims=True)
    cross = nt(feats, batch)
    dist = center_norms + batch_norms.T - 2.0 * cross
    tile = jnp.exp(-dist / SCALE).astype(jnp.bfloat16)
    spread = jnp.dot(coeffs_ref[...], tile, preferred_element_type=jnp.float32)
    pred = spread.T
    pred_mine_ref[...] = pred[:half]
    pred_other_ref[...] = pred[half:]
    local = lax.rem(land_ref[...], slab)
    lands = local.shape[0]
    chosen = lax.broadcasted_iota(jnp.int32, (lands, slab), 1) == local
    pick = jnp.where(chosen, 1.0, 0.0).astype(jnp.bfloat16)
    land_tile_ref[...] = jnp.dot(
        pick, tile, preferred_element_type=jnp.float32
    ).astype(jnp.bfloat16)


def tile_and_pred(mine, other, center_feats, coeffs_t, landmark_index):
    half, lands, out = mine.shape[0], landmark_index.shape[0], coeffs_t.shape[0]
    slab, width = center_feats.shape
    vmem = pl.BlockSpec(memory_space=pltpu.VMEM)
    return pl.pallas_call(
        tile_kernel,
        out_shape=(
            jax.ShapeDtypeStruct((half, out), jnp.float32),
            jax.ShapeDtypeStruct((half, out), jnp.float32),
            jax.ShapeDtypeStruct((lands, 2 * half), jnp.bfloat16),
        ),
        in_specs=[vmem] * 5,
        out_specs=(vmem,) * 3,
        compiler_params=pltpu.CompilerParams(vmem_limit_bytes=VMEM_LIMIT),
    )(mine, other, center_feats, coeffs_t, landmark_index.reshape(lands, 1))


def resid_kernel(parts_ref, running_ref, labels_ref, new_ref, resid_ref):
    total = running_ref[...]
    for chip in range(parts_ref.shape[0]):
        total = total + parts_ref[chip]
    new_ref[...] = total
    resid = (total - labels_ref[...].astype(jnp.float32)).astype(jnp.bfloat16)
    for chip in range(resid_ref.shape[0]):
        resid_ref[chip] = resid


def residuals(parts, running, labels):
    chips, rows, out = parts.shape
    vmem = pl.BlockSpec(memory_space=pltpu.VMEM)
    return pl.pallas_call(
        resid_kernel,
        out_shape=(
            jax.ShapeDtypeStruct((rows, out), jnp.float32),
            jax.ShapeDtypeStruct((chips, rows, out), jnp.bfloat16),
        ),
        in_specs=[vmem] * 3,
        out_specs=(vmem,) * 2,
        compiler_params=pltpu.CompilerParams(vmem_limit_bytes=VMEM_LIMIT),
    )(parts, running, labels)


def per_device(size, center_feats, coeffs, labels, running, batch_index, landmark_index):
    chips = size // 2
    swap = [(i, i ^ 1) for i in range(size)]
    across = [[core + 2 * chip for chip in range(chips)] for core in range(2)]

    def exchange(blocks):
        return lax.all_to_all(
            blocks, "centers", 0, 0, axis_index_groups=across, tiled=True
        )

    picks = batch_index.shape[0]
    own = gather_rows(center_feats, batch_index, chips)
    mine = exchange(own).reshape(chips * picks, -1)
    other = lax.ppermute(mine, "centers", swap)
    pred_mine, pred_other, land_tile = tile_and_pred(
        mine, other, center_feats, coeffs.T, landmark_index
    )
    pair = pred_mine + lax.ppermute(pred_other, "centers", swap)
    parts = exchange(pair.reshape(chips, picks, -1))
    new_running, resid = residuals(parts, running, labels)
    resid_mine = exchange(resid).reshape(chips * picks, -1)
    resid_other = lax.ppermute(resid_mine, "centers", swap)
    projection = jnp.dot(
        land_tile,
        jnp.concatenate([resid_mine, resid_other], axis=0),
        preferred_element_type=jnp.float32,
    )
    return (new_running, projection)


def solution(mesh):
    row = P(("groups", "centers"), None)
    flat = P(("groups", "centers"))
    return jax.shard_map(
        functools.partial(per_device, mesh.shape["centers"]),
        mesh=mesh,
        in_specs=(row, row, row, row, flat, flat),
        out_specs=(row, row),
        check_vma=False,
    )
```

time: 123 us -> 51.6 us (0.42)
  waiting for transfers between devices: 49.3 us -> 3.96 us
  between operations: 14.1 us -> 0.67 us
  blocking collectives: 43.9 us -> 37 us
  Pallas kernels: 0 us -> 4.25 us
  matrix products: 5.35 us -> 1.14 us
  other arithmetic: 3.83 us -> 0.03 us
  local copies, waits for them, and re-layouts: 6.35 us -> 3.94 us
    reduce_scatter x1 -> x0, waiting for transfers between devices: 49.3 us -> none  [per_device(): lax.psum_scatter(jnp.dot(tile, coeffs, preferred_element_type=jnp.float32...]
    all_gather x2 -> x0, blocking collectives: 43.9 us -> none  [the longest x1 23.8 us: per_device(): batch_feats = lax.all_gather(own_feats, 'centers', axis=0, tiled=True)]
    all_to_all x0 -> x3, blocking collectives: none -> 37 us  [exchange(): lax.all_to_all(blocks, 'centers', 0, 0, axis_index_groups=across, tiled=T...]
    gather x3 -> x0, local copies, waits for them, and re-layouts: 6.32 us -> none  [the longest x1 2.91 us: per_device(): land_feats = jnp.take(center_feats, land_local, axis=0)]
    pallas_call x0 -> x3, Pallas kernels: none -> 4.25 us  [the longest x1 2.37 us: tile_and_pred(): pl.pallas_call(tile_kernel, out_shape=(jax.ShapeDtypeStruct((half, out),...]
    dot_general x2 -> x1, matrix products: 5.35 us -> 1.14 us  [per_device(): jnp.dot(land_tile, jnp.concatenate([resid_mine, resid_other], axis=0), pr...]
    ppermute x0 -> x3, waiting for transfers between devices: none -> 3.96 us  [the longest x1 1.39 us: per_device(): pair = pred_mine + lax.ppermute(pred_other, 'centers', swap)]
    unnamed x10 -> x14, local copies, waits for them, and re-layouts: 0.03 us -> 3.83 us
  transfers between devices with their start and end apart: 1 -> 3, of which waited for: 1 -> 3; matrix products, arithmetic and copies ran while one was open for 3% -> 0% of each run, Pallas kernels for 0% -> 0%
where the time goes in v1:
time: 51.6 us; the launch traced here: 51.3 us
  blocking collectives  37 us (72%)
  Pallas kernels  4.25 us (8%)
  waiting for transfers between devices  3.96 us (8%)
  local copies, waits for them, and re-layouts  3.94 us (8%)
  matrix products  1.14 us (2%)
  between operations  0.67 us (1%)
    all_to_all x3, blocking collectives, exchange(): lax.all_to_all(blocks, 'centers', 0, 0, axis_index_groups=across, tiled=T...  37 us
    unnamed x14, local copies, waits for them, and re-layouts  3.83 us
    pallas_call x1, Pallas kernels, tile_and_pred(): pl.pallas_call(tile_kernel, out_shape=(jax.ShapeDtypeStruct((half, out),...  2.37 us
    ppermute x1, waiting for transfers between devices, per_device(): pair = pred_mine + lax.ppermute(pred_other, 'centers', swap)  1.39 us
    ppermute x1, waiting for transfers between devices, per_device(): resid_other = lax.ppermute(resid_mine, 'centers', swap)  1.35 us
    pallas_call x1, Pallas kernels, gather_rows(): pl.pallas_call(gather_kernel, out_shape=jax.ShapeDtypeStruct((chips, pick...  1.25 us
    ppermute x1, waiting for transfers between devices, per_device(): other = lax.ppermute(mine, 'centers', swap)  1.23 us
    dot_general x1, matrix products, per_device(): jnp.dot(land_tile, jnp.concatenate([resid_mine, resid_other], axis=0), pr...  1.14 us
  transfers between devices with their start and end apart: 3, of which 3 were waited for; matrix products, arithmetic and copies ran while one was open for 0% of the time, Pallas kernels for 0%

profile of v1, /device:TPU:0, one launch (start us, length us, event | category | flops | bytes accessed | tf_op | source)
XLA Modules:
  0.0 51.3 jit_solution(6848769831331820136)
XLA Ops:
  0.6 0.0 copy-start
  0.6 1.6 %copy-done = bf16[1024,1024]{1,0:T(8,128)(2,1)S(1)} copy-done((bf16[1024,1024]{1,0:T(8,128)(2,1)S(1)}, bf16[1024,1024]{1,0:T(8,128)(2,1)}, u32[]{:S(2)}) %copy-start) | copy-done | bytes 2097176
  2.2 0.0 copy-start.5
  2.2 0.7 %copy-done.5 = s32[8]{0:T(128)S(1)} copy-done((s32[8]{0:T(128)S(1)}, s32[8]{0:T(128)}, u32[]{:S(2)}) %copy-start.5) | copy-done | bytes 56
  2.9 0.0 copy-start.6
  2.9 0.0 copy-start.1
  2.9 1.2 %shard_map.77 = bf16[8,8,1024]{2,1,0:T(8,128)(2,1)S(1)} custom-call(s32[8]{0:T(128)S(1)} %copy-done.5, bf16[1024,1024]{1,0:T(8,128)(2,1)S(1)} %copy-done), custom_call_target="tpu_custom_call" | custom-call | tf_op jit(solution)/shard_map/pallas_call | solution.py:41
  4.1 14.4 %all_to_all.15 = bf16[8,8,1024]{2,1,0:T(8,128)(2,1)S(1)} all-to-all(bf16[8,8,1024]{2,1,0:T(8,128)(2,1)S(1)} %shard_map.77), channel_id=1, replica_groups={{0,2,4,6,8,10,12,14},{1,3,5,7,9,11,13,15},{16,18,20,22,24,26,28,30},{17..., dimensions={0} | all-to-all | bytes 262144 | tf_op jit(solution)/shard_map/all_to_all | solution.py:138
  18.6 0.0 collective-permute-start
  18.6 0.0 copy-done.6
  18.6 0.1 copy.8.land_ref
  18.7 1.2 %collective-permute-done.other_ref = bf16[64,1024]{1,0:T(8,128)(2,1)S(1)} collective-permute-done((bf16[64,1024]{1,0:T(8,128)(2,1)S(1)}, bf16[64,1024]{1,0:T(8,128)(2,1)S(1)}, u32[]{:S(2)}, u32[]{:S(2)}) %collective-permute-start) | collective-permute-done | bytes 131104 | tf_op jit(solution)/shard_map/ppermute | solution.py:145
  19.9 0.0 copy-done.1
  19.9 0.0 copy-start.2
  19.9 1.6 %copy-done.2 = bf16[1024,1000]{0,1:T(8,128)(2,1)S(1)} copy-done((bf16[1024,1000]{0,1:T(8,128)(2,1)S(1)}, bf16[1024,1000]{0,1:T(8,128)(2,1)}, u32[]{:S(2)}) %copy-start.2) | copy-done | bytes 2048024
  21.5 0.0 copy-start.3
  21.5 0.0 copy-start.4
  21.5 2.4 %shard_map.78 = (f32[64,1000]{1,0:T(8,128)S(1)}, f32[64,1000]{1,0:T(8,128)S(1)}, bf16[128,128]{1,0:T(8,128)(2,1)S(1)}) custom-call(bf16[64,1024]{1,0:T(8,128)(2,1)S(1)} %bitcast.9, bf16[64,1024]{1,0:T(8,128)(2,1)S(1)} %collective-permute-done.other_ref, bf16[1024,1024]{1,0:T(8,128)(2,1)S(1)} %copy-done.1, bf16[1000,1024]{1,0:T(8,128)(2,1)S(1)} %bitcast.7, ...), custom_call_target="tpu_custom_call" | custom-call | tf_op jit(solution)/shard_map/pallas_call | solution.py:94
  23.9 0.2 collective-permute-start.1
  24.1 1.4 %collective-permute-done.1 = f32[64,1000]{1,0:T(8,128)S(1)} collective-permute-done((f32[64,1000]{1,0:T(8,128)S(1)}, f32[64,1000]{1,0:T(8,128)S(1)}, u32[]{:S(2)}, u32[]{:S(2)}) %collective-permute-start.1) | collective-permute-done | bytes 256032 | tf_op jit(solution)/shard_map/ppermute | solution.py:149
  25.5 11.9 %all_to_all.16.parts_ref = f32[8,8,1000]{2,1,0:T(8,128)S(1)} all-to-all(f32[8,8,1000]{2,1,0:T(8,128)S(1)} %add_bitcast_fusion), channel_id=1, replica_groups={{0,2,4,6,8,10,12,14},{1,3,5,7,9,11,13,15},{16,18,20,22,24,26,28,30},{17..., dimensions={0} | all-to-all | bytes 512000 | tf_op jit(solution)/shard_map/all_to_all | solution.py:138
  37.4 0.0 copy-done.3
  37.4 0.0 copy-done.4
  37.4 0.6 %shard_map.79 = (f32[8,1000]{1,0:T(8,128)}, bf16[8,8,1000]{2,1,0:T(8,128)(2,1)S(1)}) custom-call(f32[8,8,1000]{2,1,0:T(8,128)S(1)} %all_to_all.16.parts_ref, f32[8,1000]{1,0:T(8,128)S(1)} %copy-done.3, bf16[8,1000]{1,0:T(8,128)(2,1)S(1)} %copy-done.4), custom_call_target="tpu_custom_call" | custom-call | tf_op jit(solution)/shard_map/pallas_call | solution.py:120
  38.1 10.7 %all_to_all.17 = bf16[8,8,1000]{2,1,0:T(8,128)(2,1)S(1)} all-to-all(bf16[8,8,1000]{2,1,0:T(8,128)(2,1)S(1)} %get-tuple-element.11), channel_id=1, replica_groups={{0,2,4,6,8,10,12,14},{1,3,5,7,9,11,13,15},{16,18,20,22,24,26,28,30},{17..., dimensions={0} | all-to-all | bytes 256000 | tf_op jit(solution)/shard_map/all_to_all | solution.py:138
  48.8 0.0 collective-permute-start.2
  48.8 1.3 %collective-permute-done.2 = bf16[64,1000]{1,0:T(8,128)(2,1)S(1)} collective-permute-done((bf16[64,1000]{1,0:T(8,128)(2,1)S(1)}, bf16[64,1000]{1,0:T(8,128)(2,1)S(1)}, u32[]{:S(2)}, u32[]{:S(2)}) %collective-permute-start.2) | collective-permute-done | bytes 128032 | tf_op jit(solution)/shard_map/ppermute | solution.py:153
  50.1 1.1 %fusion = f32[128,1000]{0,1:T(8,128)} fusion(bf16[128,128]{1,0:T(8,128)(2,1)S(1)} %get-tuple-element.10, bf16[64,1000]{1,0:T(8,128)(2,1)S(1)} %collective-permute-done.2, bf16[64,1000]{1,0:T(8,128)(2,1)S(1)} %bitcast.11), kind=kOutput, calls=%fused_computation | convolution fusion | flops 33280000 | bytes 800768 | tf_op jit(solution)/shard_map/dot_general | solution.py:154
  (1 shorter events, 0.0 us)
Async XLA Ops:
  0.6 1.6 %copy-start = (bf16[1024,1024]{1,0:T(8,128)(2,1)S(1)}, bf16[1024,1024]{1,0:T(8,128)(2,1)}, u32[]{:S(2)}) copy-start(bf16[1024,1024]{1,0:T(8,128)(2,1)} %feats_ref.3) | copy-start | bytes 6291460
  2.2 0.7 %copy-start.5 = (s32[8]{0:T(128)S(1)}, s32[8]{0:T(128)}, u32[]{:S(2)}) copy-start(s32[8]{0:T(128)} %index_ref.1) | copy-start | bytes 100
  2.9 15.7 %copy-start.6 = (s32[128]{0:T(128)S(1)}, s32[128]{0:T(128)}, u32[]{:S(2)}) copy-start(s32[128]{0:T(128)} %param.11) | copy-start | bytes 1540
  2.9 17.0 %copy-start.1 = (bf16[1024,1024]{1,0:T(8,128)(2,1)S(1)}, bf16[1024,1024]{1,0:T(8,128)(2,1)}, u32[]{:S(2)}) copy-start(bf16[1024,1024]{1,0:T(8,128)(2,1)} %feats_ref.3) | copy-start | bytes 6291460
  18.6 1.3 %collective-permute-start = (bf16[64,1024]{1,0:T(8,128)(2,1)S(1)}, bf16[64,1024]{1,0:T(8,128)(2,1)S(1)}, u32[]{:S(2)}, u32[]{:S(2)}) collective-permute-start(bf16[64,1024]{1,0:T(8,128)(2,1)S(1)} %bitcast.8), channel_id=1, source_target_pairs={{0,1},{1,0},{2,3},{3,2},{4,5},{5,4},{6,7},{7,6},{8,9},{9,8},{10,11... | collective-permute-start | bytes 393224 | tf_op jit(solution)/shard_map/ppermute | solution.py:145
  19.9 1.6 %copy-start.2 = (bf16[1024,1000]{0,1:T(8,128)(2,1)S(1)}, bf16[1024,1000]{0,1:T(8,128)(2,1)}, u32[]{:S(2)}) copy-start(bf16[1024,1000]{0,1:T(8,128)(2,1)} %param.7) | copy-start | bytes 6144004
  21.5 15.9 %copy-start.3 = (f32[8,1000]{1,0:T(8,128)S(1)}, f32[8,1000]{1,0:T(8,128)}, u32[]{:S(2)}) copy-start(f32[8,1000]{1,0:T(8,128)} %running_ref.1) | copy-start | bytes 96004
  21.5 15.9 %copy-start.4 = (bf16[8,1000]{1,0:T(8,128)(2,1)S(1)}, bf16[8,1000]{1,0:T(8,128)(2,1)}, u32[]{:S(2)}) copy-start(bf16[8,1000]{1,0:T(8,128)(2,1)} %labels_ref.1) | copy-start | bytes 48004
  23.9 1.6 %collective-permute-start.1 = (f32[64,1000]{1,0:T(8,128)S(1)}, f32[64,1000]{1,0:T(8,128)S(1)}, u32[]{:S(2)}, u32[]{:S(2)}) collective-permute-start(f32[64,1000]{1,0:T(8,128)S(1)} %get-tuple-element.8), channel_id=1, source_target_pairs={{0,1},{1,0},{2,3},{3,2},{4,5},{5,4},{6,7},{7,6},{8,9},{9,8},{10,11... | collective-permute-start | bytes 768008 | tf_op jit(solution)/shard_map/ppermute | solution.py:149
  48.8 1.3 %collective-permute-start.2 = (bf16[64,1000]{1,0:T(8,128)(2,1)S(1)}, bf16[64,1000]{1,0:T(8,128)(2,1)S(1)}, u32[]{:S(2)}, u32[]{:S(2)}) collective-permute-start(bf16[64,1000]{1,0:T(8,128)(2,1)S(1)} %bitcast.10), channel_id=1, source_target_pairs={{0,1},{1,0},{2,3},{3,2},{4,5},{5,4},{6,7},{7,6},{8,9},{9,8},{10,11... | collective-permute-start | bytes 384008 | tf_op jit(solution)/shard_map/ppermute | solution.py:153

commit v2 on v1

v2 whole, which is shorter than its diff:
```python
import functools

import jax
import jax.numpy as jnp
from jax import lax
from jax.experimental import pallas as pl
from jax.experimental.pallas import tpu as pltpu
from jax.sharding import PartitionSpec as P

SCALE = 1024.0
VMEM_LIMIT = 16 * 1024 * 1024


def gather_kernel(index_ref, feats_ref, out_ref, rows):
    for i in range(index_ref.shape[0]):
        row = index_ref[i]
        start = pl.multiple_of((row // 16) * 16, 16)
        block = feats_ref[pl.ds(start, 16), :].astype(jnp.float32)
        here = lax.broadcasted_iota(jnp.int32, block.shape, 0) == row - start
        rows[i : i + 1, :] = jnp.sum(jnp.where(here, block, 0.0), axis=0, keepdims=True)
    picked = rows[...].astype(out_ref.dtype)
    for chip in range(out_ref.shape[0]):
        out_ref[chip] = picked


def gather_rows(center_feats, batch_index, chips):
    picks, width = batch_index.shape[0], center_feats.shape[1]
    vmem = pl.BlockSpec(memory_space=pltpu.VMEM)
    return pl.pallas_call(
        gather_kernel,
        out_shape=jax.ShapeDtypeStruct((chips, picks, width), center_feats.dtype),
        in_specs=[pl.BlockSpec(memory_space=pltpu.SMEM), vmem],
        out_specs=vmem,
        scratch_shapes=[pltpu.VMEM((picks, width), jnp.float32)],
        compiler_params=pltpu.CompilerParams(vmem_limit_bytes=VMEM_LIMIT),
    )(batch_index, center_feats)


def nt(a, b):
    return lax.dot_general(
        a, b, (((1,), (1,)), ((), ())), preferred_element_type=jnp.float32
    )


def tile_kernel(mine_ref, other_ref, feats_ref, land_ref, tile_ref, land_tile_ref):
    slab = feats_ref.shape[0]
    batch = jnp.concatenate([mine_ref[...], other_ref[...]], axis=0)
    feats = feats_ref[...]
    wide = feats.astype(jnp.float32)
    center_norms = jnp.sum(wide * wide, axis=1, keepdims=True)
    batch_wide = batch.astype(jnp.float32)
    batch_norms = jnp.sum(batch_wide * batch_wide, axis=1, keepdims=True)
    dist = center_norms + batch_norms.T - 2.0 * nt(feats, batch)
    tile = jnp.exp(-dist / SCALE).astype(jnp.bfloat16)
    tile_ref[...] = tile
    local = land_ref[...]
    chosen = lax.broadcasted_iota(jnp.int32, (local.shape[0], slab), 1) == local
    pick = jnp.where(chosen, 1.0, 0.0).astype(jnp.bfloat16)
    land_tile_ref[...] = jnp.dot(
        pick, tile, preferred_element_type=jnp.float32
    ).astype(jnp.bfloat16)


def kernel_tiles(mine, other, center_feats, land_local):
    half, lands, slab = mine.shape[0], land_local.shape[0], center_feats.shape[0]
    vmem = pl.BlockSpec(memory_space=pltpu.VMEM)
    return pl.pallas_call(
        tile_kernel,
        out_shape=(
            jax.ShapeDtypeStruct((slab, 2 * half), jnp.bfloat16),
            jax.ShapeDtypeStruct((lands, 2 * half), jnp.bfloat16),
        ),
        in_specs=[vmem] * 4,
        out_specs=(vmem,) * 2,
        compiler_params=pltpu.CompilerParams(
            vmem_limit_bytes=VMEM_LIMIT * (1 if half <= 64 else 3)
        ),
    )(mine, other, center_feats, land_local.reshape(lands, 1))


def pred_kernel(tile_ref, coeffs_ref, mine_ref, other_ref):
    pred = jnp.dot(
        coeffs_ref[...], tile_ref[...], preferred_element_type=jnp.float32
    ).T
    half = mine_ref.shape[0]
    mine_ref[...] = pred[:half]
    other_ref[...] = pred[half:]


def predictions(tile, coeffs_t):
    half, out = tile.shape[1] // 2, coeffs_t.shape[0]
    vmem = pl.BlockSpec(memory_space=pltpu.VMEM)
    return pl.pallas_call(
        pred_kernel,
        out_shape=(jax.ShapeDtypeStruct((half, out), jnp.float32),) * 2,
        in_specs=[vmem] * 2,
        out_specs=(vmem,) * 2,
        compiler_params=pltpu.CompilerParams(
            vmem_limit_bytes=VMEM_LIMIT * (1 if half <= 64 else 3)
        ),
    )(tile, coeffs_t)


def resid_kernel(parts_ref, running_ref, labels_ref, new_ref, resid_ref):
    total = running_ref[...]
    for chip in range(parts_ref.shape[0]):
        total = total + parts_ref[chip]
    new_ref[...] = total
    resid = (total - labels_ref[...].astype(jnp.float32)).astype(jnp.bfloat16)
    for chip in range(resid_ref.shape[0]):
        resid_ref[chip] = resid


def residuals(parts, running, labels):
    chips, rows, out = parts.shape
    vmem = pl.BlockSpec(memory_space=pltpu.VMEM)
    return pl.pallas_call(
        resid_kernel,
        out_shape=(
            jax.ShapeDtypeStruct((rows, out), jnp.float32),
            jax.ShapeDtypeStruct((chips, rows, out), jnp.bfloat16),
        ),
        in_specs=[vmem] * 3,
        out_specs=(vmem,) * 2,
        compiler_params=pltpu.CompilerParams(vmem_limit_bytes=VMEM_LIMIT),
    )(parts, running, labels)


def per_device(size, center_feats, coeffs, labels, running, batch_index, landmark_index):
    chips = size // 2
    swap = [(i, i ^ 1) for i in range(size)]
    across = [[core + 2 * chip for chip in range(chips)] for core in range(2)]

    def exchange(blocks):
        return lax.all_to_all(
            blocks, "centers", 0, 0, axis_index_groups=across, tiled=True
        )

    picks = batch_index.shape[0]
    slab = center_feats.shape[0]
    own = gather_rows(center_feats, lax.rem(batch_index, slab), chips)
    mine = exchange(own).reshape(chips * picks, -1)
    other = lax.ppermute(mine, "centers", swap)
    tile, land_tile = kernel_tiles(
        mine, other, center_feats, lax.rem(landmark_index, slab)
    )
    pred_mine, pred_other = predictions(tile, coeffs.T)
    pair = pred_mine + lax.ppermute(pred_other, "centers", swap)
    parts = exchange(pair.reshape(chips, picks, -1))
    new_running, resid = residuals(parts, running, labels)
    resid_mine = exchange(resid).reshape(chips * picks, -1)
    resid_other = lax.ppermute(resid_mine, "centers", swap)
    projection = jnp.dot(
        land_tile,
        jnp.concatenate([resid_mine, resid_other], axis=0),
        preferred_element_type=jnp.float32,
    )
    return (new_running, projection)


def solution(mesh):
    row = P(("groups", "centers"), None)
    flat = P(("groups", "centers"))
    return jax.shard_map(
        functools.partial(per_device, mesh.shape["centers"]),
        mesh=mesh,
        in_specs=(row, row, row, row, flat, flat),
        out_specs=(row, row),
        check_vma=False,
    )
```

time: 51.6 us -> 48.9 us (0.948)
  local copies, waits for them, and re-layouts: 3.94 us -> 1.73 us
  Pallas kernels: 4.25 us -> 3.17 us
  other arithmetic: 0.03 us -> 0.72 us
    unnamed x14 -> x12, local copies, waits for them, and re-layouts: 3.83 us -> 1.61 us
    rem x0 -> x1, other arithmetic: none -> 0.67 us  [per_device(): own = gather_rows(center_feats, lax.rem(batch_index, slab), chips)]
    pallas_call x1, Pallas kernels: 1.25 us -> 0.68 us  [gather_rows(): pl.pallas_call(gather_kernel, out_shape=jax.ShapeDtypeStruct((chips, pick...]
    pallas_call x1 -> x2, Pallas kernels: 2.37 us -> 1.85 us  [the longest x1 1.09 us: kernel_tiles(): pl.pallas_call(tile_kernel, out_shape=(jax.ShapeDtypeStruct((slab, 2 * ha...]
where the time goes in v2:
time: 48.9 us; the launch traced here: 48.7 us
  blocking collectives  37 us (76%)
  waiting for transfers between devices  3.95 us (8%)
  Pallas kernels  3.17 us (6%)
  local copies, waits for them, and re-layouts  1.73 us (4%)
  matrix products  1.14 us (2%)
  other arithmetic  0.72 us (1%)
  between operations  0.69 us (1%)
    all_to_all x3, blocking collectives, exchange(): lax.all_to_all(blocks, 'centers', 0, 0, axis_index_groups=across, tiled=T...  37 us
    unnamed x12, local copies, waits for them, and re-layouts  1.61 us
    ppermute x1, waiting for transfers between devices, per_device(): pair = pred_mine + lax.ppermute(pred_other, 'centers', swap)  1.39 us
    ppermute x1, waiting for transfers between devices, per_device(): resid_other = lax.ppermute(resid_mine, 'centers', swap)  1.35 us
    ppermute x1, waiting for transfers between devices, per_device(): other = lax.ppermute(mine, 'centers', swap)  1.21 us
    dot_general x1, matrix products, per_device(): jnp.dot(land_tile, jnp.concatenate([resid_mine, resid_other], axis=0), pr...  1.14 us
    pallas_call x1, Pallas kernels, kernel_tiles(): pl.pallas_call(tile_kernel, out_shape=(jax.ShapeDtypeStruct((slab, 2 * ha...  1.09 us
  transfers between devices with their start and end apart: 3, of which 3 were waited for; matrix products, arithmetic and copies ran while one was open for 0% of the time, Pallas kernels for 0%

profile of v2, /device:TPU:0, one launch (start us, length us, event | category | flops | bytes accessed | tf_op | source)
XLA Modules:
  0.0 48.7 jit_solution(17497825566229339492)
XLA Ops:
  0.6 0.0 copy-start.5
  0.6 0.7 %compare_select_fusion.2.index_ref = s32[8]{0:T(128)S(1)} fusion(s32[8]{0:T(128)} %param.10), kind=kLoop, calls=%fused_computation.7 | loop fusion | flops 48 | bytes 64 | tf_op jit(solution)/shard_map/rem | solution.py:141
  1.3 0.0 copy-start
  1.3 1.6 %copy-done = bf16[1024,1024]{1,0:T(8,128)(2,1)S(1)} copy-done((bf16[1024,1024]{1,0:T(8,128)(2,1)S(1)}, bf16[1024,1024]{1,0:T(8,128)(2,1)}, u32[]{:S(2)}) %copy-start) | copy-done | bytes 2097176
  2.9 0.0 copy-start.1
  2.9 0.7 %shard_map.77 = bf16[8,8,1024]{2,1,0:T(8,128)(2,1)S(1)} custom-call(s32[8]{0:T(128)S(1)} %compare_select_fusion.2.index_ref, bf16[1024,1024]{1,0:T(8,128)(2,1)S(1)} %copy-done), custom_call_target="tpu_custom_call" | custom-call | tf_op jit(solution)/shard_map/pallas_call | solution.py:29
  3.6 14.4 %all_to_all.15 = bf16[8,8,1024]{2,1,0:T(8,128)(2,1)S(1)} all-to-all(bf16[8,8,1024]{2,1,0:T(8,128)(2,1)S(1)} %shard_map.77), channel_id=1, replica_groups={{0,2,4,6,8,10,12,14},{1,3,5,7,9,11,13,15},{16,18,20,22,24,26,28,30},{17..., dimensions={0} | all-to-all | bytes 262144 | tf_op jit(solution)/shard_map/all_to_all | solution.py:135
  18.0 0.0 collective-permute-start
  18.0 0.0 copy-done.5
  18.0 0.1 copy.8.land_ref
  18.1 0.0 copy-start.2
  18.1 1.2 %collective-permute-done.other_ref = bf16[64,1024]{1,0:T(8,128)(2,1)S(1)} collective-permute-done((bf16[64,1024]{1,0:T(8,128)(2,1)S(1)}, bf16[64,1024]{1,0:T(8,128)(2,1)S(1)}, u32[]{:S(2)}, u32[]{:S(2)}) %collective-permute-start) | collective-permute-done | bytes 131104 | tf_op jit(solution)/shard_map/ppermute | solution.py:143
  19.4 0.0 copy-done.1
  19.4 1.1 %shard_map.78 = (bf16[1024,128]{1,0:T(8,128)(2,1)S(1)}, bf16[128,128]{1,0:T(8,128)(2,1)S(1)}) custom-call(bf16[64,1024]{1,0:T(8,128)(2,1)S(1)} %bitcast.10, bf16[64,1024]{1,0:T(8,128)(2,1)S(1)} %collective-permute-done.other_ref, bf16[1024,1024]{1,0:T(8,128)(2,1)S(1)} %copy-done.1, s32[128,1]{1,0:T(8,128)S(1)} %copy.8.land_ref), custom_call_target="tpu_custom_call" | custom-call | tf_op jit(solution)/shard_map/pallas_call | solution.py:67
  20.5 0.0 copy-start.3
  20.5 0.0 copy-start.4
  20.5 0.0 copy-done.2
  20.5 0.8 %shard_map.79 = (f32[64,1000]{1,0:T(8,128)S(1)}, f32[64,1000]{1,0:T(8,128)S(1)}) custom-call(bf16[1024,128]{1,0:T(8,128)(2,1)S(1)} %get-tuple-element.8.tile_ref, bf16[1000,1024]{1,0:T(8,128)(2,1)S(1)} %bitcast.8), custom_call_target="tpu_custom_call" | custom-call | tf_op jit(solution)/shard_map/pallas_call | solution.py:93
  21.3 0.2 collective-permute-start.1
  21.5 1.4 %collective-permute-done.1 = f32[64,1000]{1,0:T(8,128)S(1)} collective-permute-done((f32[64,1000]{1,0:T(8,128)S(1)}, f32[64,1000]{1,0:T(8,128)S(1)}, u32[]{:S(2)}, u32[]{:S(2)}) %collective-permute-start.1) | collective-permute-done | bytes 256032 | tf_op jit(solution)/shard_map/ppermute | solution.py:148
  22.9 11.9 %all_to_all.16.parts_ref = f32[8,8,1000]{2,1,0:T(8,128)S(1)} all-to-all(f32[8,8,1000]{2,1,0:T(8,128)S(1)} %add_bitcast_fusion), channel_id=1, replica_groups={{0,2,4,6,8,10,12,14},{1,3,5,7,9,11,13,15},{16,18,20,22,24,26,28,30},{17..., dimensions={0} | all-to-all | bytes 512000 | tf_op jit(solution)/shard_map/all_to_all | solution.py:135
  34.8 0.0 copy-done.3
  34.8 0.0 copy-done.4
  34.8 0.6 %shard_map.80 = (f32[8,1000]{1,0:T(8,128)}, bf16[8,8,1000]{2,1,0:T(8,128)(2,1)S(1)}) custom-call(f32[8,8,1000]{2,1,0:T(8,128)S(1)} %all_to_all.16.parts_ref, f32[8,1000]{1,0:T(8,128)S(1)} %copy-done.3, bf16[8,1000]{1,0:T(8,128)(2,1)S(1)} %copy-done.4), custom_call_target="tpu_custom_call" | custom-call | tf_op jit(solution)/shard_map/pallas_call | solution.py:117
  35.5 10.7 %all_to_all.17 = bf16[8,8,1000]{2,1,0:T(8,128)(2,1)S(1)} all-to-all(bf16[8,8,1000]{2,1,0:T(8,128)(2,1)S(1)} %get-tuple-element.13), channel_id=1, replica_groups={{0,2,4,6,8,10,12,14},{1,3,5,7,9,11,13,15},{16,18,20,22,24,26,28,30},{17..., dimensions={0} | all-to-all | bytes 256000 | tf_op jit(solution)/shard_map/all_to_all | solution.py:135
  46.2 0.0 collective-permute-start.2
  46.2 1.3 %collective-permute-done.2 = bf16[64,1000]{1,0:T(8,128)(2,1)S(1)} collective-permute-done((bf16[64,1000]{1,0:T(8,128)(2,1)S(1)}, bf16[64,1000]{1,0:T(8,128)(2,1)S(1)}, u32[]{:S(2)}, u32[]{:S(2)}) %collective-permute-start.2) | collective-permute-done | bytes 128032 | tf_op jit(solution)/shard_map/ppermute | solution.py:152
  47.5 1.1 %fusion = f32[128,1000]{0,1:T(8,128)} fusion(bf16[128,128]{1,0:T(8,128)(2,1)S(1)} %get-tuple-element.12, bf16[64,1000]{1,0:T(8,128)(2,1)S(1)} %collective-permute-done.2, bf16[64,1000]{1,0:T(8,128)(2,1)S(1)} %bitcast.12), kind=kOutput, calls=%fused_computation | convolution fusion | flops 33280000 | bytes 800768 | tf_op jit(solution)/shard_map/dot_general | solution.py:153
  (2 shorter events, 0.0 us)
Async XLA Ops:
  0.6 17.4 %copy-start.5 = (s32[128]{0:T(128)S(1)}, s32[128]{0:T(128)}, u32[]{:S(2)}) copy-start(s32[128]{0:T(128)} %param.11) | copy-start | bytes 1540
  1.3 1.6 %copy-start = (bf16[1024,1024]{1,0:T(8,128)(2,1)S(1)}, bf16[1024,1024]{1,0:T(8,128)(2,1)}, u32[]{:S(2)}) copy-start(bf16[1024,1024]{1,0:T(8,128)(2,1)} %feats_ref.3) | copy-start | bytes 6291460
  2.9 16.5 %copy-start.1 = (bf16[1024,1024]{1,0:T(8,128)(2,1)S(1)}, bf16[1024,1024]{1,0:T(8,128)(2,1)}, u32[]{:S(2)}) copy-start(bf16[1024,1024]{1,0:T(8,128)(2,1)} %feats_ref.3) | copy-start | bytes 6291460
  18.0 1.3 %collective-permute-start = (bf16[64,1024]{1,0:T(8,128)(2,1)S(1)}, bf16[64,1024]{1,0:T(8,128)(2,1)S(1)}, u32[]{:S(2)}, u32[]{:S(2)}) collective-permute-start(bf16[64,1024]{1,0:T(8,128)(2,1)S(1)} %bitcast.9), channel_id=1, source_target_pairs={{0,1},{1,0},{2,3},{3,2},{4,5},{5,4},{6,7},{7,6},{8,9},{9,8},{10,11... | collective-permute-start | bytes 393224 | tf_op jit(solution)/shard_map/ppermute | solution.py:143
  18.1 2.3 %copy-start.2 = (bf16[1024,1000]{0,1:T(8,128)(2,1)S(1)}, bf16[1024,1000]{0,1:T(8,128)(2,1)}, u32[]{:S(2)}) copy-start(bf16[1024,1000]{0,1:T(8,128)(2,1)} %param.7) | copy-start | bytes 6144004
  20.5 14.4 %copy-start.3 = (f32[8,1000]{1,0:T(8,128)S(1)}, f32[8,1000]{1,0:T(8,128)}, u32[]{:S(2)}) copy-start(f32[8,1000]{1,0:T(8,128)} %running_ref.1) | copy-start | bytes 96004
  20.5 14.4 %copy-start.4 = (bf16[8,1000]{1,0:T(8,128)(2,1)S(1)}, bf16[8,1000]{1,0:T(8,128)(2,1)}, u32[]{:S(2)}) copy-start(bf16[8,1000]{1,0:T(8,128)(2,1)} %labels_ref.1) | copy-start | bytes 48004
  21.3 1.6 %collective-permute-start.1 = (f32[64,1000]{1,0:T(8,128)S(1)}, f32[64,1000]{1,0:T(8,128)S(1)}, u32[]{:S(2)}, u32[]{:S(2)}) collective-permute-start(f32[64,1000]{1,0:T(8,128)S(1)} %get-tuple-element.10), channel_id=1, source_target_pairs={{0,1},{1,0},{2,3},{3,2},{4,5},{5,4},{6,7},{7,6},{8,9},{9,8},{10,11... | collective-permute-start | bytes 768008 | tf_op jit(solution)/shard_map/ppermute | solution.py:148
  46.2 1.3 %collective-permute-start.2 = (bf16[64,1000]{1,0:T(8,128)(2,1)S(1)}, bf16[64,1000]{1,0:T(8,128)(2,1)S(1)}, u32[]{:S(2)}, u32[]{:S(2)}) collective-permute-start(bf16[64,1000]{1,0:T(8,128)(2,1)S(1)} %bitcast.11), channel_id=1, source_target_pairs={{0,1},{1,0},{2,3},{3,2},{4,5},{5,4},{6,7},{7,6},{8,9},{9,8},{10,11... | collective-permute-start | bytes 384008 | tf_op jit(solution)/shard_map/ppermute | solution.py:152

commit v3 on v2

--- a/solution.py
+++ b/solution.py
@@ -8,6 +8,7 @@
 from jax.sharding import PartitionSpec as P
 
 SCALE = 1024.0
+SENT_SCALE = 128.0
 VMEM_LIMIT = 16 * 1024 * 1024
 
 
@@ -146,8 +147,11 @@
     )
     pred_mine, pred_other = predictions(tile, coeffs.T)
     pair = pred_mine + lax.ppermute(pred_other, "centers", swap)
-    parts = exchange(pair.reshape(chips, picks, -1))
-    new_running, resid = residuals(parts, running, labels)
+    sent = (pair * SENT_SCALE).astype(jnp.float16)
+    parts = exchange(sent.reshape(chips, picks, -1)).astype(jnp.float32)
+    new_running = running + jnp.sum(parts, axis=0) / SENT_SCALE
+    resid = (new_running - labels.astype(jnp.float32)).astype(jnp.bfloat16)
+    resid = jnp.broadcast_to(resid, (chips,) + resid.shape)
     resid_mine = exchange(resid).reshape(chips * picks, -1)
     resid_other = lax.ppermute(resid_mine, "centers", swap)
     projection = jnp.dot(

time: 48.9 us -> 46.2 us (0.945)
  blocking collectives: 37 us -> 34.2 us
  other arithmetic: 0.72 us -> 1.37 us
  Pallas kernels: 3.17 us -> 2.53 us
    all_to_all x3, blocking collectives: 37 us -> 34.2 us  [exchange(): lax.all_to_all(blocks, 'centers', 0, 0, axis_index_groups=across, tiled=T...]
    pallas_call x1 -> x0, Pallas kernels: 0.64 us -> none  [residuals(): pl.pallas_call(resid_kernel, out_shape=(jax.ShapeDtypeStruct((rows, out),...]
    convert_element_type x0 -> x1, other arithmetic: none -> 0.62 us  [per_device(): resid = (new_running - labels.astype(jnp.float32)).astype(jnp.bfloat16)]
where the time goes in v3:
time: 46.2 us; the launch traced here: 45.9 us
  blocking collectives  34.2 us (74%)
  waiting for transfers between devices  3.95 us (9%)
  Pallas kernels  2.53 us (5%)
  local copies, waits for them, and re-layouts  1.74 us (4%)
  other arithmetic  1.37 us (3%)
  matrix products  1.14 us (2%)
  between operations  0.71 us (2%)
    all_to_all x3, blocking collectives, exchange(): lax.all_to_all(blocks, 'centers', 0, 0, axis_index_groups=across, tiled=T...  34.2 us
    unnamed x12, local copies, waits for them, and re-layouts  1.61 us
    ppermute x1, waiting for transfers between devices, per_device(): pair = pred_mine + lax.ppermute(pred_other, 'centers', swap)  1.39 us
    ppermute x1, waiting for transfers between devices, per_device(): resid_other = lax.ppermute(resid_mine, 'centers', swap)  1.35 us
    ppermute x1, waiting for transfers between devices, per_device(): other = lax.ppermute(mine, 'centers', swap)  1.21 us
    dot_general x1, matrix products, per_device(): jnp.dot(land_tile, jnp.concatenate([resid_mine, resid_other], axis=0), pr...  1.14 us
    pallas_call x1, Pallas kernels, kernel_tiles(): pl.pallas_call(tile_kernel, out_shape=(jax.ShapeDtypeStruct((slab, 2 * ha...  1.09 us
  transfers between devices with their start and end apart: 3, of which 3 were waited for; matrix products, arithmetic and copies ran while one was open for 0% of the time, Pallas kernels for 0%

profile of v3, /device:TPU:0, one launch (start us, length us, event | category | flops | bytes accessed | tf_op | source)
XLA Modules:
  0.0 45.9 jit_solution(3318428435674914294)
XLA Ops:
  0.6 0.0 copy-start.5
  0.6 0.7 %compare_select_fusion.2.index_ref = s32[8]{0:T(128)S(1)} fusion(s32[8]{0:T(128)} %param.10), kind=kLoop, calls=%fused_computation.11 | loop fusion | flops 48 | bytes 64 | tf_op jit(solution)/shard_map/rem | solution.py:142
  1.3 0.0 copy-start
  1.3 1.6 %copy-done = bf16[1024,1024]{1,0:T(8,128)(2,1)S(1)} copy-done((bf16[1024,1024]{1,0:T(8,128)(2,1)S(1)}, bf16[1024,1024]{1,0:T(8,128)(2,1)}, u32[]{:S(2)}) %copy-start) | copy-done | bytes 2097176
  2.9 0.0 copy-start.1
  2.9 0.7 %shard_map.77 = bf16[8,8,1024]{2,1,0:T(8,128)(2,1)S(1)} custom-call(s32[8]{0:T(128)S(1)} %compare_select_fusion.2.index_ref, bf16[1024,1024]{1,0:T(8,128)(2,1)S(1)} %copy-done), custom_call_target="tpu_custom_call" | custom-call | tf_op jit(solution)/shard_map/pallas_call | solution.py:30
  3.6 14.4 %all_to_all.15 = bf16[8,8,1024]{2,1,0:T(8,128)(2,1)S(1)} all-to-all(bf16[8,8,1024]{2,1,0:T(8,128)(2,1)S(1)} %shard_map.77), channel_id=1, replica_groups={{0,2,4,6,8,10,12,14},{1,3,5,7,9,11,13,15},{16,18,20,22,24,26,28,30},{17..., dimensions={0} | all-to-all | bytes 262144 | tf_op jit(solution)/shard_map/all_to_all | solution.py:136
  18.0 0.0 collective-permute-start
  18.0 0.0 copy-done.5
  18.0 0.1 copy.8.land_ref
  18.1 0.0 copy-start.2
  18.1 1.2 %collective-permute-done.other_ref = bf16[64,1024]{1,0:T(8,128)(2,1)S(1)} collective-permute-done((bf16[64,1024]{1,0:T(8,128)(2,1)S(1)}, bf16[64,1024]{1,0:T(8,128)(2,1)S(1)}, u32[]{:S(2)}, u32[]{:S(2)}) %collective-permute-start) | collective-permute-done | bytes 131104 | tf_op jit(solution)/shard_map/ppermute | solution.py:144
  19.4 0.0 copy-done.1
  19.4 1.1 %shard_map.78 = (bf16[1024,128]{1,0:T(8,128)(2,1)S(1)}, bf16[128,128]{1,0:T(8,128)(2,1)S(1)}) custom-call(bf16[64,1024]{1,0:T(8,128)(2,1)S(1)} %bitcast.10, bf16[64,1024]{1,0:T(8,128)(2,1)S(1)} %collective-permute-done.other_ref, bf16[1024,1024]{1,0:T(8,128)(2,1)S(1)} %copy-done.1, s32[128,1]{1,0:T(8,128)S(1)} %copy.8.land_ref), custom_call_target="tpu_custom_call" | custom-call | tf_op jit(solution)/shard_map/pallas_call | solution.py:68
  20.5 0.0 copy-start.3
  20.5 0.0 copy-start.4
  20.5 0.0 copy-done.2
  20.5 0.8 %shard_map.79 = (f32[64,1000]{1,0:T(8,128)S(1)}, f32[64,1000]{1,0:T(8,128)S(1)}) custom-call(bf16[1024,128]{1,0:T(8,128)(2,1)S(1)} %get-tuple-element.6.tile_ref, bf16[1000,1024]{1,0:T(8,128)(2,1)S(1)} %bitcast.8), custom_call_target="tpu_custom_call" | custom-call | tf_op jit(solution)/shard_map/pallas_call | solution.py:94
  21.3 0.2 collective-permute-start.1
  21.5 1.4 %collective-permute-done.1 = f32[64,1000]{1,0:T(8,128)S(1)} collective-permute-done((f32[64,1000]{1,0:T(8,128)S(1)}, f32[64,1000]{1,0:T(8,128)S(1)}, u32[]{:S(2)}, u32[]{:S(2)}) %collective-permute-start.1) | collective-permute-done | bytes 256032 | tf_op jit(solution)/shard_map/ppermute | solution.py:149
  22.9 10.0 %all_to_all.16 = f16[8,8,1000]{2,1,0:T(8,128)(2,1)S(1)} all-to-all(f16[8,8,1000]{2,1,0:T(8,128)(2,1)S(1)} %fusion.4), channel_id=1, replica_groups={{0,2,4,6,8,10,12,14},{1,3,5,7,9,11,13,15},{16,18,20,22,24,26,28,30},{17..., dimensions={0} | all-to-all | bytes 256000 | tf_op jit(solution)/shard_map/all_to_all | solution.py:136
  32.9 0.0 copy-done.3
  32.9 0.0 copy-done.4
  32.9 0.6 %subtract_convert_fusion = (bf16[8,1000]{1,0:T(8,128)(2,1)S(1)}, f32[8,1000]{1,0:T(8,128)}) fusion(bf16[8,1000]{1,0:T(8,128)(2,1)S(1)} %copy-done.4, f32[8,1000]{1,0:T(8,128)S(1)} %copy-done.3, f32[8,1000]{1,0:T(8,128)S(1)} %convert_reduce_fusion), kind=kLoop, calls=%fused_computation.7 | loop fusion | flops 40000 | bytes 128000 | tf_op jit(solution)/shard_map/convert_element_type | solution.py:153
  33.6 9.8 %all_to_all.17 = bf16[8,8,1000]{2,1,0:T(8,128)(2,1)S(1)} all-to-all(bf16[8,8,1000]{2,1,0:T(8,128)(2,1)S(1)} %broadcast_in_dim.3), channel_id=1, replica_groups={{0,2,4,6,8,10,12,14},{1,3,5,7,9,11,13,15},{16,18,20,22,24,26,28,30},{17..., dimensions={0} | all-to-all | bytes 256000 | tf_op jit(solution)/shard_map/all_to_all | solution.py:136
  43.4 0.0 collective-permute-start.2
  43.4 1.3 %collective-permute-done.2 = bf16[64,1000]{1,0:T(8,128)(2,1)S(1)} collective-permute-done((bf16[64,1000]{1,0:T(8,128)(2,1)S(1)}, bf16[64,1000]{1,0:T(8,128)(2,1)S(1)}, u32[]{:S(2)}, u32[]{:S(2)}) %collective-permute-start.2) | collective-permute-done | bytes 128032 | tf_op jit(solution)/shard_map/ppermute | solution.py:156
  44.7 1.1 %fusion = f32[128,1000]{0,1:T(8,128)} fusion(bf16[128,128]{1,0:T(8,128)(2,1)S(1)} %get-tuple-element.9, bf16[64,1000]{1,0:T(8,128)(2,1)S(1)} %collective-permute-done.2, bf16[64,1000]{1,0:T(8,128)(2,1)S(1)} %bitcast.12), kind=kOutput, calls=%fused_computation | convolution fusion | flops 33280000 | bytes 800768 | tf_op jit(solution)/shard_map/dot_general | solution.py:157
  (4 shorter events, 0.1 us)
Async XLA Ops:
  0.6 17.4 %copy-start.5 = (s32[128]{0:T(128)S(1)}, s32[128]{0:T(128)}, u32[]{:S(2)}) copy-start(s32[128]{0:T(128)} %param.11) | copy-start | bytes 1540
  1.3 1.6 %copy-start = (bf16[1024,1024]{1,0:T(8,128)(2,1)S(1)}, bf16[1024,1024]{1,0:T(8,128)(2,1)}, u32[]{:S(2)}) copy-start(bf16[1024,1024]{1,0:T(8,128)(2,1)} %feats_ref.3) | copy-start | bytes 6291460
  2.9 16.5 %copy-start.1 = (bf16[1024,1024]{1,0:T(8,128)(2,1)S(1)}, bf16[1024,1024]{1,0:T(8,128)(2,1)}, u32[]{:S(2)}) copy-start(bf16[1024,1024]{1,0:T(8,128)(2,1)} %feats_ref.3) | copy-start | bytes 6291460
  18.0 1.3 %collective-permute-start = (bf16[64,1024]{1,0:T(8,128)(2,1)S(1)}, bf16[64,1024]{1,0:T(8,128)(2,1)S(1)}, u32[]{:S(2)}, u32[]{:S(2)}) collective-permute-start(bf16[64,1024]{1,0:T(8,128)(2,1)S(1)} %bitcast.9), channel_id=1, source_target_pairs={{0,1},{1,0},{2,3},{3,2},{4,5},{5,4},{6,7},{7,6},{8,9},{9,8},{10,11... | collective-permute-start | bytes 393224 | tf_op jit(solution)/shard_map/ppermute | solution.py:144
  18.1 2.3 %copy-start.2 = (bf16[1024,1000]{0,1:T(8,128)(2,1)S(1)}, bf16[1024,1000]{0,1:T(8,128)(2,1)}, u32[]{:S(2)}) copy-start(bf16[1024,1000]{0,1:T(8,128)(2,1)} %param.7) | copy-start | bytes 6144004
  20.5 12.4 %copy-start.3 = (f32[8,1000]{1,0:T(8,128)S(1)}, f32[8,1000]{1,0:T(8,128)}, u32[]{:S(2)}) copy-start(f32[8,1000]{1,0:T(8,128)} %param.9) | copy-start | bytes 96004
  20.5 12.4 %copy-start.4 = (bf16[8,1000]{1,0:T(8,128)(2,1)S(1)}, bf16[8,1000]{1,0:T(8,128)(2,1)}, u32[]{:S(2)}) copy-start(bf16[8,1000]{1,0:T(8,128)(2,1)} %param.8) | copy-start | bytes 48004
  21.3 1.6 %collective-permute-start.1 = (f32[64,1000]{1,0:T(8,128)S(1)}, f32[64,1000]{1,0:T(8,128)S(1)}, u32[]{:S(2)}, u32[]{:S(2)}) collective-permute-start(f32[64,1000]{1,0:T(8,128)S(1)} %get-tuple-element.8), channel_id=1, source_target_pairs={{0,1},{1,0},{2,3},{3,2},{4,5},{5,4},{6,7},{7,6},{8,9},{9,8},{10,11... | collective-permute-start | bytes 768008 | tf_op jit(solution)/shard_map/ppermute | solution.py:149
  43.4 1.3 %collective-permute-start.2 = (bf16[64,1000]{1,0:T(8,128)(2,1)S(1)}, bf16[64,1000]{1,0:T(8,128)(2,1)S(1)}, u32[]{:S(2)}, u32[]{:S(2)}) collective-permute-start(bf16[64,1000]{1,0:T(8,128)(2,1)S(1)} %bitcast.11), channel_id=1, source_target_pairs={{0,1},{1,0},{2,3},{3,2},{4,5},{5,4},{6,7},{7,6},{8,9},{9,8},{10,11... | collective-permute-start | bytes 384008 | tf_op jit(solution)/shard_map/ppermute | solution.py:156

commit v4 on v3

v4 whole, which is shorter than its diff:
```python
import functools

import jax
import jax.numpy as jnp
from jax import lax
from jax.experimental import pallas as pl
from jax.experimental.pallas import tpu as pltpu
from jax.sharding import PartitionSpec as P

SCALE = 1024.0
SENT_SCALE = 128.0
VMEM_LIMIT = 16 * 1024 * 1024


def vmem_limit(half):
    return pltpu.CompilerParams(vmem_limit_bytes=VMEM_LIMIT * (1 if half <= 64 else 3))


def local_kernel(slab, index_ref, out_ref):
    out_ref[...] = lax.rem(index_ref[...], slab)


def local_index(index, slab):
    vmem = pl.BlockSpec(memory_space=pltpu.VMEM)
    return pl.pallas_call(
        functools.partial(local_kernel, slab),
        out_shape=jax.ShapeDtypeStruct(index.shape, index.dtype),
        in_specs=[vmem],
        out_specs=vmem,
        compiler_params=pltpu.CompilerParams(vmem_limit_bytes=VMEM_LIMIT),
    )(index)


def gather_kernel(index_ref, feats_ref, out_ref, rows):
    for i in range(index_ref.shape[0]):
        row = index_ref[i]
        start = pl.multiple_of((row // 16) * 16, 16)
        block = feats_ref[pl.ds(start, 16), :].astype(jnp.float32)
        here = lax.broadcasted_iota(jnp.int32, block.shape, 0) == row - start
        rows[i : i + 1, :] = jnp.sum(jnp.where(here, block, 0.0), axis=0, keepdims=True)
    picked = rows[...].astype(out_ref.dtype)
    for chip in range(out_ref.shape[0]):
        out_ref[chip] = picked


def gather_rows(center_feats, batch_index, chips):
    picks, width = batch_index.shape[0], center_feats.shape[1]
    vmem = pl.BlockSpec(memory_space=pltpu.VMEM)
    return pl.pallas_call(
        gather_kernel,
        out_shape=jax.ShapeDtypeStruct((chips, picks, width), center_feats.dtype),
        in_specs=[pl.BlockSpec(memory_space=pltpu.SMEM), vmem],
        out_specs=vmem,
        scratch_shapes=[pltpu.VMEM((picks, width), jnp.float32)],
        compiler_params=pltpu.CompilerParams(vmem_limit_bytes=VMEM_LIMIT),
    )(batch_index, center_feats)


def nt(a, b):
    return lax.dot_general(
        a, b, (((1,), (1,)), ((), ())), preferred_element_type=jnp.float32
    )


def norm_kernel(mine_ref, feats_ref, centers_ref, mine_norms_ref):
    feats = feats_ref[...].astype(jnp.float32)
    centers_ref[...] = jnp.sum(feats * feats, axis=1, keepdims=True)
    mine = mine_ref[...].astype(jnp.float32)
    mine_norms_ref[...] = jnp.sum(mine * mine, axis=1, keepdims=True)


def norms(mine, center_feats):
    vmem = pl.BlockSpec(memory_space=pltpu.VMEM)
    return pl.pallas_call(
        norm_kernel,
        out_shape=(
            jax.ShapeDtypeStruct((center_feats.shape[0], 1), jnp.float32),
            jax.ShapeDtypeStruct((mine.shape[0], 1), jnp.float32),
        ),
        in_specs=[vmem] * 2,
        out_specs=(vmem,) * 2,
        compiler_params=vmem_limit(mine.shape[0]),
    )(mine, center_feats)


def tile_kernel(mine_ref, other_ref, feats_ref, centers_ref, mine_norms_ref, tile_ref):
    other = other_ref[...]
    batch = jnp.concatenate([mine_ref[...], other], axis=0)
    wide = other.astype(jnp.float32)
    other_norms = jnp.sum(wide * wide, axis=1, keepdims=True)
    batch_norms = jnp.concatenate([mine_norms_ref[...], other_norms], axis=0)
    dist = centers_ref[...] + batch_norms.T - 2.0 * nt(feats_ref[...], batch)
    tile_ref[...] = jnp.exp(-dist / SCALE).astype(jnp.bfloat16)


def kernel_tile(mine, other, center_feats, center_norms, mine_norms):
    half, slab = mine.shape[0], center_feats.shape[0]
    vmem = pl.BlockSpec(memory_space=pltpu.VMEM)
    return pl.pallas_call(
        tile_kernel,
        out_shape=jax.ShapeDtypeStruct((slab, 2 * half), jnp.bfloat16),
        in_specs=[vmem] * 5,
        out_specs=vmem,
        compiler_params=vmem_limit(half),
    )(mine, other, center_feats, center_norms, mine_norms)


def land_kernel(tile_ref, land_ref, land_tile_ref):
    tile = tile_ref[...]
    shape = (land_ref.shape[0], tile.shape[0])
    chosen = lax.broadcasted_iota(jnp.int32, shape, 1) == land_ref[...]
    pick = jnp.where(chosen, 1.0, 0.0).astype(jnp.bfloat16)
    land_tile_ref[...] = jnp.dot(
        pick, tile, preferred_element_type=jnp.float32
    ).astype(jnp.bfloat16)


def land_rows(tile, land_local):
    lands = land_local.shape[0]
    vmem = pl.BlockSpec(memory_space=pltpu.VMEM)
    return pl.pallas_call(
        land_kernel,
        out_shape=jax.ShapeDtypeStruct((lands, tile.shape[1]), jnp.bfloat16),
        in_specs=[vmem] * 2,
        out_specs=vmem,
        compiler_params=vmem_limit(tile.shape[1] // 2),
    )(tile, land_local.reshape(lands, 1))


def pred_kernel(tile_ref, coeffs_ref, mine_ref, other_ref):
    pred = jnp.dot(
        coeffs_ref[...], tile_ref[...], preferred_element_type=jnp.float32
    ).T
    half = mine_ref.shape[0]
    mine_ref[...] = pred[:half]
    other_ref[...] = pred[half:]


def predictions(tile, coeffs_t):
    half, out = tile.shape[1] // 2, coeffs_t.shape[0]
    vmem = pl.BlockSpec(memory_space=pltpu.VMEM)
    return pl.pallas_call(
        pred_kernel,
        out_shape=(jax.ShapeDtypeStruct((half, out), jnp.float32),) * 2,
        in_specs=[vmem] * 2,
        out_specs=(vmem,) * 2,
        compiler_params=vmem_limit(half),
    )(tile, coeffs_t)


def per_device(size, center_feats, coeffs, labels, running, batch_index, landmark_index):
    chips = size // 2
    swap = [(i, i ^ 1) for i in range(size)]
    across = [[2 * chip + (chip.bit_count() + core) % 2 for chip in range(chips)] for core in range(2)]

    def exchange(blocks):
        return lax.all_to_all(
            blocks, "centers", 0, 0, axis_index_groups=across, tiled=True
        )

    picks = batch_index.shape[0]
    slab = center_feats.shape[0]
    own = gather_rows(center_feats, local_index(batch_index, slab), chips)
    mine = exchange(own).reshape(chips * picks, -1)
    other = lax.ppermute(mine, "centers", swap)
    center_norms, mine_norms = norms(mine, center_feats)
    tile = kernel_tile(mine, other, center_feats, center_norms, mine_norms)
    pred_mine, pred_other = predictions(tile, coeffs.T)
    land_tile = land_rows(tile, lax.rem(landmark_index, slab))
    pair = pred_mine + lax.ppermute(pred_other, "centers", swap)
    sent = (pair * SENT_SCALE).astype(jnp.float16)
    parts = exchange(sent.reshape(chips, picks, -1)).astype(jnp.float32)
    new_running = running + jnp.sum(parts, axis=0) / SENT_SCALE
    resid = (new_running - labels.astype(jnp.float32)).astype(jnp.bfloat16)
    resid = jnp.broadcast_to(resid, (chips,) + resid.shape)
    resid_mine = exchange(resid).reshape(chips * picks, -1)
    resid_other = lax.ppermute(resid_mine, "centers", swap)
    projection = jnp.dot(
        land_tile,
        jnp.concatenate([resid_mine, resid_other], axis=0),
        preferred_element_type=jnp.float32,
    )
    return (new_running, projection)


def solution(mesh):
    row = P(("groups", "centers"), None)
    flat = P(("groups", "centers"))
    return jax.shard_map(
        functools.partial(per_device, mesh.shape["centers"]),
        mesh=mesh,
        in_specs=(row, row, row, row, flat, flat),
        out_specs=(row, row),
        check_vma=False,
    )
```

time: 46.2 us -> 45.3 us (0.981)
  waiting for transfers between devices: 3.95 us -> 2.51 us
  blocking collectives: 34.2 us -> 33 us
  starting transfers between devices: 0.22 us -> 1.27 us
  local copies, waits for them, and re-layouts: 1.74 us -> 2.66 us
  other arithmetic: 1.37 us -> 0.7 us
  Pallas kernels: 2.53 us -> 3 us
    all_to_all x3, blocking collectives: 34.2 us -> 33 us  [exchange(): lax.all_to_all(blocks, 'centers', 0, 0, axis_index_groups=across, tiled=T...]
    unnamed x12 -> x14, local copies, waits for them, and re-layouts: 1.61 us -> 2.54 us
    ppermute x1, waiting for transfers between devices: 1.35 us -> 0.57 us  [per_device(): resid_other = lax.ppermute(resid_mine, 'centers', swap)]
    ppermute x1, waiting for transfers between devices: 1.21 us -> 0.49 us  [per_device(): other = lax.ppermute(mine, 'centers', swap)]
    ppermute x1, starting transfers between devices: 0.01 us -> 0.68 us  [per_device(): other = lax.ppermute(mine, 'centers', swap)]
    rem x1 -> x0, other arithmetic: 0.67 us -> none  [per_device(): own = gather_rows(center_feats, lax.rem(batch_index, slab), chips)]
    pallas_call x1 -> x4, Pallas kernels: 1.09 us -> 1.55 us  [the longest x1 0.77 us: kernel_tile(): pl.pallas_call(tile_kernel, out_shape=jax.ShapeDtypeStruct((slab, 2 * hal...]
  transfers between devices with their start and end apart: 3 -> 3, of which waited for: 3 -> 3; matrix products, arithmetic and copies ran while one was open for 0% -> 0% of each run, Pallas kernels for 0% -> 2%
where the time goes in v4:
time: 45.3 us; the launch traced here: 45 us
  blocking collectives  33 us (73%)
  Pallas kernels  3 us (7%)
  local copies, waits for them, and re-layouts  2.66 us (6%)
  waiting for transfers between devices  2.51 us (6%)
  starting transfers between devices  1.27 us (3%)
  matrix products  1.14 us (3%)
  between operations  0.71 us (2%)
  other arithmetic  0.7 us (2%)
    all_to_all x3, blocking collectives, exchange(): lax.all_to_all(blocks, 'centers', 0, 0, axis_index_groups=across, tiled=T...  33 us
    unnamed x14, local copies, waits for them, and re-layouts  2.54 us
    ppermute x1, waiting for transfers between devices, per_device(): pair = pred_mine + lax.ppermute(pred_other, 'centers', swap)  1.45 us
    dot_general x1, matrix products, per_device(): jnp.dot(land_tile, jnp.concatenate([resid_mine, resid_other], axis=0), pr...  1.14 us
  transfers between devices with their start and end apart: 3, of which 3 were waited for; matrix products, arithmetic and copies ran while one was open for 0% of the time, Pallas kernels for 2%

profile of v4, /device:TPU:0, one launch (start us, length us, event | category | flops | bytes accessed | tf_op | source)
XLA Modules:
  0.0 45.0 jit_solution(9241887845990018632)
XLA Ops:
  0.6 0.0 copy-start.3
  0.6 0.6 %copy-done.3 = s32[8]{0:T(128)S(1)} copy-done((s32[8]{0:T(128)S(1)}, s32[8]{0:T(128)}, u32[]{:S(2)}) %copy-start.3) | copy-done | bytes 56
  1.3 0.0 copy-start
  1.3 1.6 %copy-done = bf16[1024,1024]{1,0:T(8,128)(2,1)S(1)} copy-done((bf16[1024,1024]{1,0:T(8,128)(2,1)S(1)}, bf16[1024,1024]{1,0:T(8,128)(2,1)}, u32[]{:S(2)}) %copy-start) | copy-done | bytes 2097176
  2.9 0.0 copy-start.1
  2.9 0.7 %shard_map.78 = bf16[8,8,1024]{2,1,0:T(8,128)(2,1)S(1)} custom-call(s32[8]{0:T(128)S(1)} %shard_map.77.index_ref, bf16[1024,1024]{1,0:T(8,128)(2,1)S(1)} %copy-done), custom_call_target="tpu_custom_call" | custom-call | tf_op jit(solution)/shard_map/pallas_call | solution.py:49
  3.6 13.5 %all_to_all.15 = bf16[8,8,1024]{2,1,0:T(8,128)(2,1)S(1)} all-to-all(bf16[8,8,1024]{2,1,0:T(8,128)(2,1)S(1)} %shard_map.78), channel_id=1, replica_groups={{0,3,5,6,9,10,12,15},{1,2,4,7,8,11,13,14},{16,19,21,22,25,26,28,31},{17..., dimensions={0} | all-to-all | bytes 262144 | tf_op jit(solution)/shard_map/all_to_all | solution.py:157
  17.1 0.7 %collective-permute-start = (bf16[64,1024]{1,0:T(8,128)(2,1)S(1)}, bf16[64,1024]{1,0:T(8,128)(2,1)S(1)}, u32[]{:S(2)}, u32[]{:S(2)}) collective-permute-start(bf16[64,1024]{1,0:T(8,128)(2,1)S(1)} %bitcast.9), channel_id=1, source_target_pairs={{0,1},{1,0},{2,3},{3,2},{4,5},{5,4},{6,7},{7,6},{8,9},{9,8},{10,11... | collective-permute-start | bytes 393224 | tf_op jit(solution)/shard_map/ppermute | solution.py:165
  17.7 0.0 copy-done.1
  17.7 0.5 %shard_map.79 = (f32[1024,1]{1,0:T(8,128)S(1)}, f32[64,1]{1,0:T(8,128)S(1)}) custom-call(bf16[64,1024]{1,0:T(8,128)(2,1)S(1)} %bitcast.10, bf16[1024,1024]{1,0:T(8,128)(2,1)S(1)} %copy-done.1), custom_call_target="tpu_custom_call" | custom-call | tf_op jit(solution)/shard_map/pallas_call | solution.py:74
  18.2 0.0 copy-start.2
  18.2 0.5 %collective-permute-done.other_ref = bf16[64,1024]{1,0:T(8,128)(2,1)S(1)} collective-permute-done((bf16[64,1024]{1,0:T(8,128)(2,1)S(1)}, bf16[64,1024]{1,0:T(8,128)(2,1)S(1)}, u32[]{:S(2)}, u32[]{:S(2)}) %collective-permute-start) | collective-permute-done | bytes 131104 | tf_op jit(solution)/shard_map/ppermute | solution.py:165
  18.7 0.8 %shard_map.80.tile_ref = bf16[1024,128]{1,0:T(8,128)(2,1)S(1)} custom-call(bf16[64,1024]{1,0:T(8,128)(2,1)S(1)} %bitcast.11, bf16[64,1024]{1,0:T(8,128)(2,1)S(1)} %collective-permute-done.other_ref, bf16[1024,1024]{1,0:T(8,128)(2,1)S(1)} %copy-done.1, f32[1024,1]{1,0:T(8,128)S(1)} %get-tuple-element.6.centers_ref, f32[64,1]{1,0:T(8,128)S(1)} %get-tuple-element.7.mine_norms_ref), custom_call_target="tpu_custom_call" | custom-call | tf_op jit(solution)/shard_map/pallas_call | solution.py:99
  19.5 0.0 copy-start.4
  19.5 0.0 copy-start.5
  19.5 0.0 copy-start.6
  19.5 0.3 copy-done.2
  19.8 0.8 %shard_map.81 = (f32[64,1000]{1,0:T(8,128)S(1)}, f32[64,1000]{1,0:T(8,128)S(1)}) custom-call(bf16[1024,128]{1,0:T(8,128)(2,1)S(1)} %shard_map.80.tile_ref, bf16[1000,1024]{1,0:T(8,128)(2,1)S(1)} %bitcast.8), custom_call_target="tpu_custom_call" | custom-call | tf_op jit(solution)/shard_map/pallas_call | solution.py:142
  20.6 0.2 collective-permute-start.1
  20.7 1.4 %collective-permute-done.1 = f32[64,1000]{1,0:T(8,128)S(1)} collective-permute-done((f32[64,1000]{1,0:T(8,128)S(1)}, f32[64,1000]{1,0:T(8,128)S(1)}, u32[]{:S(2)}, u32[]{:S(2)}) %collective-permute-start.1) | collective-permute-done | bytes 256032 | tf_op jit(solution)/shard_map/ppermute | solution.py:170
  22.2 9.9 %all_to_all.16 = f16[8,8,1000]{2,1,0:T(8,128)(2,1)S(1)} all-to-all(f16[8,8,1000]{2,1,0:T(8,128)(2,1)S(1)} %fusion.4), channel_id=1, replica_groups={{0,3,5,6,9,10,12,15},{1,2,4,7,8,11,13,14},{16,19,21,22,25,26,28,31},{17..., dimensions={0} | all-to-all | bytes 256000 | tf_op jit(solution)/shard_map/all_to_all | solution.py:157
  32.2 0.0 copy-done.4
  32.2 0.0 copy-done.5
  32.2 0.6 %subtract_convert_fusion = (bf16[8,1000]{1,0:T(8,128)(2,1)S(1)}, f32[8,1000]{1,0:T(8,128)}) fusion(bf16[8,1000]{1,0:T(8,128)(2,1)S(1)} %copy-done.5, f32[8,1000]{1,0:T(8,128)S(1)} %copy-done.4, f32[8,1000]{1,0:T(8,128)S(1)} %convert_reduce_fusion), kind=kLoop, calls=%fused_computation.7 | loop fusion | flops 40000 | bytes 128000 | tf_op jit(solution)/shard_map/convert_element_type | solution.py:174
  32.8 9.6 %all_to_all.17 = bf16[8,8,1000]{2,1,0:T(8,128)(2,1)S(1)} all-to-all(bf16[8,8,1000]{2,1,0:T(8,128)(2,1)S(1)} %broadcast_in_dim.3), channel_id=1, replica_groups={{0,3,5,6,9,10,12,15},{1,2,4,7,8,11,13,14},{16,19,21,22,25,26,28,31},{17..., dimensions={0} | all-to-all | bytes 256000 | tf_op jit(solution)/shard_map/all_to_all | solution.py:157
  42.4 0.4 collective-permute-start.2
  42.9 0.0 copy-done.6
  42.9 0.1 copy.8.land_ref
  43.0 0.3 shard_map.82
  43.3 0.6 %collective-permute-done.2 = bf16[64,1000]{1,0:T(8,128)(2,1)S(1)} collective-permute-done((bf16[64,1000]{1,0:T(8,128)(2,1)S(1)}, bf16[64,1000]{1,0:T(8,128)(2,1)S(1)}, u32[]{:S(2)}, u32[]{:S(2)}) %collective-permute-start.2) | collective-permute-done | bytes 128032 | tf_op jit(solution)/shard_map/ppermute | solution.py:177
  43.9 1.1 %fusion = f32[128,1000]{0,1:T(8,128)} fusion(bf16[128,128]{1,0:T(8,128)(2,1)S(1)} %shard_map.82, bf16[64,1000]{1,0:T(8,128)(2,1)S(1)} %collective-permute-done.2, bf16[64,1000]{1,0:T(8,128)(2,1)S(1)} %bitcast.13), kind=kOutput, calls=%fused_computation | convolution fusion | flops 33280000 | bytes 800768 | tf_op jit(solution)/shard_map/dot_general | solution.py:178
  (5 shorter events, 0.1 us)
Async XLA Ops:
  0.6 0.7 %copy-start.3 = (s32[8]{0:T(128)S(1)}, s32[8]{0:T(128)}, u32[]{:S(2)}) copy-start(s32[8]{0:T(128)} %index_ref.1) | copy-start | bytes 100
  1.3 1.6 %copy-start = (bf16[1024,1024]{1,0:T(8,128)(2,1)S(1)}, bf16[1024,1024]{1,0:T(8,128)(2,1)}, u32[]{:S(2)}) copy-start(bf16[1024,1024]{1,0:T(8,128)(2,1)} %feats_ref.5) | copy-start | bytes 6291460
  2.9 14.9 %copy-start.1 = (bf16[1024,1024]{1,0:T(8,128)(2,1)S(1)}, bf16[1024,1024]{1,0:T(8,128)(2,1)}, u32[]{:S(2)}) copy-start(bf16[1024,1024]{1,0:T(8,128)(2,1)} %feats_ref.5) | copy-start | bytes 6291460
  17.1 1.7 %collective-permute-start = (bf16[64,1024]{1,0:T(8,128)(2,1)S(1)}, bf16[64,1024]{1,0:T(8,128)(2,1)S(1)}, u32[]{:S(2)}, u32[]{:S(2)}) collective-permute-start(bf16[64,1024]{1,0:T(8,128)(2,1)S(1)} %bitcast.9), channel_id=1, source_target_pairs={{0,1},{1,0},{2,3},{3,2},{4,5},{5,4},{6,7},{7,6},{8,9},{9,8},{10,11... | collective-permute-start | bytes 393224 | tf_op jit(solution)/shard_map/ppermute | solution.py:165
  18.2 1.6 %copy-start.2 = (bf16[1024,1000]{0,1:T(8,128)(2,1)S(1)}, bf16[1024,1000]{0,1:T(8,128)(2,1)}, u32[]{:S(2)}) copy-start(bf16[1024,1000]{0,1:T(8,128)(2,1)} %param.7) | copy-start | bytes 6144004
  19.5 12.7 %copy-start.4 = (f32[8,1000]{1,0:T(8,128)S(1)}, f32[8,1000]{1,0:T(8,128)}, u32[]{:S(2)}) copy-start(f32[8,1000]{1,0:T(8,128)} %param.9) | copy-start | bytes 96004
  19.5 12.7 %copy-start.5 = (bf16[8,1000]{1,0:T(8,128)(2,1)S(1)}, bf16[8,1000]{1,0:T(8,128)(2,1)}, u32[]{:S(2)}) copy-start(bf16[8,1000]{1,0:T(8,128)(2,1)} %param.8) | copy-start | bytes 48004
  19.5 23.4 %copy-start.6 = (s32[128]{0:T(128)S(1)}, s32[128]{0:T(128)}, u32[]{:S(2)}) copy-start(s32[128]{0:T(128)} %param.11) | copy-start | bytes 1540
  20.6 1.6 %collective-permute-start.1 = (f32[64,1000]{1,0:T(8,128)S(1)}, f32[64,1000]{1,0:T(8,128)S(1)}, u32[]{:S(2)}, u32[]{:S(2)}) collective-permute-start(f32[64,1000]{1,0:T(8,128)S(1)} %get-tuple-element.9), channel_id=1, source_target_pairs={{0,1},{1,0},{2,3},{3,2},{4,5},{5,4},{6,7},{7,6},{8,9},{9,8},{10,11... | collective-permute-start | bytes 768008 | tf_op jit(solution)/shard_map/ppermute | solution.py:170
  42.4 1.4 %collective-permute-start.2 = (bf16[64,1000]{1,0:T(8,128)(2,1)S(1)}, bf16[64,1000]{1,0:T(8,128)(2,1)S(1)}, u32[]{:S(2)}, u32[]{:S(2)}) collective-permute-start(bf16[64,1000]{1,0:T(8,128)(2,1)S(1)} %bitcast.12), channel_id=1, source_target_pairs={{0,1},{1,0},{2,3},{3,2},{4,5},{5,4},{6,7},{7,6},{8,9},{9,8},{10,11... | collective-permute-start | bytes 384008 | tf_op jit(solution)/shard_map/ppermute | solution.py:177

commit v5 on v4

--- a/solution.py
+++ b/solution.py
@@ -9,6 +9,7 @@
 
 SCALE = 1024.0
 SENT_SCALE = 128.0
+LONG = 10**10
 VMEM_LIMIT = 16 * 1024 * 1024
 
 
@@ -28,6 +29,7 @@
         in_specs=[vmem],
         out_specs=vmem,
         compiler_params=pltpu.CompilerParams(vmem_limit_bytes=VMEM_LIMIT),
+        cost_estimate=pl.CostEstimate(flops=LONG, bytes_accessed=0, transcendentals=0),
     )(index)
 
 

time: 45.3 us -> 44.6 us (0.985)
  local copies, waits for them, and re-layouts: 2.66 us -> 2 us
    unnamed x14 -> x12, local copies, waits for them, and re-layouts: 2.54 us -> 1.88 us
where the time goes in v5:
time: 44.6 us; the launch traced here: 44.4 us
  blocking collectives  33 us (74%)
  Pallas kernels  2.99 us (7%)
  waiting for transfers between devices  2.5 us (6%)
  local copies, waits for them, and re-layouts  2 us (4%)
  starting transfers between devices  1.28 us (3%)
  matrix products  1.14 us (3%)
  between operations  0.72 us (2%)
  other arithmetic  0.7 us (2%)
    all_to_all x3, blocking collectives, exchange(): lax.all_to_all(blocks, 'centers', 0, 0, axis_index_groups=across, tiled=T...  33 us
    unnamed x12, local copies, waits for them, and re-layouts  1.88 us
    ppermute x1, waiting for transfers between devices, per_device(): pair = pred_mine + lax.ppermute(pred_other, 'centers', swap)  1.44 us
    dot_general x1, matrix products, per_device(): jnp.dot(land_tile, jnp.concatenate([resid_mine, resid_other], axis=0), pr...  1.14 us
  transfers between devices with their start and end apart: 3, of which 3 were waited for; matrix products, arithmetic and copies ran while one was open for 0% of the time, Pallas kernels for 2%

profile of v5, /device:TPU:0, one launch (start us, length us, event | category | flops | bytes accessed | tf_op | source)
XLA Modules:
  0.0 44.4 jit_solution(6963730522291043276)
XLA Ops:
  0.6 0.0 copy-start
  0.6 0.0 copy-start.2
  0.6 0.8 %copy-done.2 = s32[8]{0:T(128)S(1)} copy-done((s32[8]{0:T(128)S(1)}, s32[8]{0:T(128)}, u32[]{:S(2)}) %copy-start.2) | copy-done | bytes 56
  1.5 0.8 %copy-done = bf16[1024,1024]{1,0:T(8,128)(2,1)S(1)} copy-done((bf16[1024,1024]{1,0:T(8,128)(2,1)S(1)}, bf16[1024,1024]{1,0:T(8,128)(2,1)}, u32[]{:S(2)}) %copy-start) | copy-done | bytes 2097176
  2.2 0.7 %shard_map.78 = bf16[8,8,1024]{2,1,0:T(8,128)(2,1)S(1)} custom-call(s32[8]{0:T(128)S(1)} %shard_map.77.index_ref, bf16[1024,1024]{1,0:T(8,128)(2,1)S(1)} %copy-done), custom_call_target="tpu_custom_call" | custom-call | tf_op jit(solution)/shard_map/pallas_call | solution.py:51
  2.9 13.5 %all_to_all.15 = bf16[8,8,1024]{2,1,0:T(8,128)(2,1)S(1)} all-to-all(bf16[8,8,1024]{2,1,0:T(8,128)(2,1)S(1)} %shard_map.78), channel_id=1, replica_groups={{0,3,5,6,9,10,12,15},{1,2,4,7,8,11,13,14},{16,19,21,22,25,26,28,31},{17..., dimensions={0} | all-to-all | bytes 262144 | tf_op jit(solution)/shard_map/all_to_all | solution.py:159
  16.4 0.7 %collective-permute-start = (bf16[64,1024]{1,0:T(8,128)(2,1)S(1)}, bf16[64,1024]{1,0:T(8,128)(2,1)S(1)}, u32[]{:S(2)}, u32[]{:S(2)}) collective-permute-start(bf16[64,1024]{1,0:T(8,128)(2,1)S(1)} %bitcast.9), channel_id=1, source_target_pairs={{0,1},{1,0},{2,3},{3,2},{4,5},{5,4},{6,7},{7,6},{8,9},{9,8},{10,11... | collective-permute-start | bytes 393224 | tf_op jit(solution)/shard_map/ppermute | solution.py:167
  17.1 0.5 %shard_map.79 = (f32[1024,1]{1,0:T(8,128)S(1)}, f32[64,1]{1,0:T(8,128)S(1)}) custom-call(bf16[64,1024]{1,0:T(8,128)(2,1)S(1)} %bitcast.10, bf16[1024,1024]{1,0:T(8,128)(2,1)S(1)} %copy-done), custom_call_target="tpu_custom_call" | custom-call | tf_op jit(solution)/shard_map/pallas_call | solution.py:76
  17.6 0.0 copy-start.1
  17.6 0.5 %collective-permute-done.other_ref = bf16[64,1024]{1,0:T(8,128)(2,1)S(1)} collective-permute-done((bf16[64,1024]{1,0:T(8,128)(2,1)S(1)}, bf16[64,1024]{1,0:T(8,128)(2,1)S(1)}, u32[]{:S(2)}, u32[]{:S(2)}) %collective-permute-start) | collective-permute-done | bytes 131104 | tf_op jit(solution)/shard_map/ppermute | solution.py:167
  18.1 0.8 %shard_map.80.tile_ref = bf16[1024,128]{1,0:T(8,128)(2,1)S(1)} custom-call(bf16[64,1024]{1,0:T(8,128)(2,1)S(1)} %bitcast.11, bf16[64,1024]{1,0:T(8,128)(2,1)S(1)} %collective-permute-done.other_ref, bf16[1024,1024]{1,0:T(8,128)(2,1)S(1)} %copy-done, f32[1024,1]{1,0:T(8,128)S(1)} %get-tuple-element.6.centers_ref, f32[64,1]{1,0:T(8,128)S(1)} %get-tuple-element.7.mine_norms_ref), custom_call_target="tpu_custom_call" | custom-call | tf_op jit(solution)/shard_map/pallas_call | solution.py:101
  18.8 0.0 copy-start.3
  18.9 0.0 copy-start.4
  18.9 0.0 copy-start.5
  18.9 0.3 copy-done.1
  19.2 0.8 %shard_map.81 = (f32[64,1000]{1,0:T(8,128)S(1)}, f32[64,1000]{1,0:T(8,128)S(1)}) custom-call(bf16[1024,128]{1,0:T(8,128)(2,1)S(1)} %shard_map.80.tile_ref, bf16[1000,1024]{1,0:T(8,128)(2,1)S(1)} %bitcast.8), custom_call_target="tpu_custom_call" | custom-call | tf_op jit(solution)/shard_map/pallas_call | solution.py:144
  19.9 0.2 collective-permute-start.1
  20.1 1.4 %collective-permute-done.1 = f32[64,1000]{1,0:T(8,128)S(1)} collective-permute-done((f32[64,1000]{1,0:T(8,128)S(1)}, f32[64,1000]{1,0:T(8,128)S(1)}, u32[]{:S(2)}, u32[]{:S(2)}) %collective-permute-start.1) | collective-permute-done | bytes 256032 | tf_op jit(solution)/shard_map/ppermute | solution.py:172
  21.6 9.9 %all_to_all.16 = f16[8,8,1000]{2,1,0:T(8,128)(2,1)S(1)} all-to-all(f16[8,8,1000]{2,1,0:T(8,128)(2,1)S(1)} %fusion.4), channel_id=1, replica_groups={{0,3,5,6,9,10,12,15},{1,2,4,7,8,11,13,14},{16,19,21,22,25,26,28,31},{17..., dimensions={0} | all-to-all | bytes 256000 | tf_op jit(solution)/shard_map/all_to_all | solution.py:159
  31.5 0.0 copy-done.3
  31.5 0.0 copy-done.4
  31.6 0.6 %subtract_convert_fusion = (bf16[8,1000]{1,0:T(8,128)(2,1)S(1)}, f32[8,1000]{1,0:T(8,128)}) fusion(bf16[8,1000]{1,0:T(8,128)(2,1)S(1)} %copy-done.4, f32[8,1000]{1,0:T(8,128)S(1)} %copy-done.3, f32[8,1000]{1,0:T(8,128)S(1)} %convert_reduce_fusion), kind=kLoop, calls=%fused_computation.7 | loop fusion | flops 40000 | bytes 128000 | tf_op jit(solution)/shard_map/convert_element_type | solution.py:176
  32.2 9.6 %all_to_all.17 = bf16[8,8,1000]{2,1,0:T(8,128)(2,1)S(1)} all-to-all(bf16[8,8,1000]{2,1,0:T(8,128)(2,1)S(1)} %broadcast_in_dim.3), channel_id=1, replica_groups={{0,3,5,6,9,10,12,15},{1,2,4,7,8,11,13,14},{16,19,21,22,25,26,28,31},{17..., dimensions={0} | all-to-all | bytes 256000 | tf_op jit(solution)/shard_map/all_to_all | solution.py:159
  41.8 0.4 collective-permute-start.2
  42.2 0.0 copy-done.5
  42.2 0.1 copy.8.land_ref
  42.4 0.3 shard_map.82
  42.6 0.6 %collective-permute-done.2 = bf16[64,1000]{1,0:T(8,128)(2,1)S(1)} collective-permute-done((bf16[64,1000]{1,0:T(8,128)(2,1)S(1)}, bf16[64,1000]{1,0:T(8,128)(2,1)S(1)}, u32[]{:S(2)}, u32[]{:S(2)}) %collective-permute-start.2) | collective-permute-done | bytes 128032 | tf_op jit(solution)/shard_map/ppermute | solution.py:179
  43.2 1.1 %fusion = f32[128,1000]{0,1:T(8,128)} fusion(bf16[128,128]{1,0:T(8,128)(2,1)S(1)} %shard_map.82, bf16[64,1000]{1,0:T(8,128)(2,1)S(1)} %collective-permute-done.2, bf16[64,1000]{1,0:T(8,128)(2,1)S(1)} %bitcast.13), kind=kOutput, calls=%fused_computation | convolution fusion | flops 33280000 | bytes 800768 | tf_op jit(solution)/shard_map/dot_general | solution.py:180
  (5 shorter events, 0.1 us)
Async XLA Ops:
  0.6 1.6 %copy-start = (bf16[1024,1024]{1,0:T(8,128)(2,1)S(1)}, bf16[1024,1024]{1,0:T(8,128)(2,1)}, u32[]{:S(2)}) copy-start(bf16[1024,1024]{1,0:T(8,128)(2,1)} %feats_ref.5) | copy-start | bytes 6291460
  0.6 0.8 %copy-start.2 = (s32[8]{0:T(128)S(1)}, s32[8]{0:T(128)}, u32[]{:S(2)}) copy-start(s32[8]{0:T(128)} %index_ref.1) | copy-start | bytes 100
  16.4 1.7 %collective-permute-start = (bf16[64,1024]{1,0:T(8,128)(2,1)S(1)}, bf16[64,1024]{1,0:T(8,128)(2,1)S(1)}, u32[]{:S(2)}, u32[]{:S(2)}) collective-permute-start(bf16[64,1024]{1,0:T(8,128)(2,1)S(1)} %bitcast.9), channel_id=1, source_target_pairs={{0,1},{1,0},{2,3},{3,2},{4,5},{5,4},{6,7},{7,6},{8,9},{9,8},{10,11... | collective-permute-start | bytes 393224 | tf_op jit(solution)/shard_map/ppermute | solution.py:167
  17.6 1.6 %copy-start.1 = (bf16[1024,1000]{0,1:T(8,128)(2,1)S(1)}, bf16[1024,1000]{0,1:T(8,128)(2,1)}, u32[]{:S(2)}) copy-start(bf16[1024,1000]{0,1:T(8,128)(2,1)} %param.7) | copy-start | bytes 6144004
  18.8 12.7 %copy-start.3 = (f32[8,1000]{1,0:T(8,128)S(1)}, f32[8,1000]{1,0:T(8,128)}, u32[]{:S(2)}) copy-start(f32[8,1000]{1,0:T(8,128)} %param.9) | copy-start | bytes 96004
  18.9 12.7 %copy-start.4 = (bf16[8,1000]{1,0:T(8,128)(2,1)S(1)}, bf16[8,1000]{1,0:T(8,128)(2,1)}, u32[]{:S(2)}) copy-start(bf16[8,1000]{1,0:T(8,128)(2,1)} %param.8) | copy-start | bytes 48004
  18.9 23.4 %copy-start.5 = (s32[128]{0:T(128)S(1)}, s32[128]{0:T(128)}, u32[]{:S(2)}) copy-start(s32[128]{0:T(128)} %param.11) | copy-start | bytes 1540
  19.9 1.6 %collective-permute-start.1 = (f32[64,1000]{1,0:T(8,128)S(1)}, f32[64,1000]{1,0:T(8,128)S(1)}, u32[]{:S(2)}, u32[]{:S(2)}) collective-permute-start(f32[64,1000]{1,0:T(8,128)S(1)} %get-tuple-element.9), channel_id=1, source_target_pairs={{0,1},{1,0},{2,3},{3,2},{4,5},{5,4},{6,7},{7,6},{8,9},{9,8},{10,11... | collective-permute-start | bytes 768008 | tf_op jit(solution)/shard_map/ppermute | solution.py:172
  41.8 1.4 %collective-permute-start.2 = (bf16[64,1000]{1,0:T(8,128)(2,1)S(1)}, bf16[64,1000]{1,0:T(8,128)(2,1)S(1)}, u32[]{:S(2)}, u32[]{:S(2)}) collective-permute-start(bf16[64,1000]{1,0:T(8,128)(2,1)S(1)} %bitcast.12), channel_id=1, source_target_pairs={{0,1},{1,0},{2,3},{3,2},{4,5},{5,4},{6,7},{7,6},{8,9},{9,8},{10,11... | collective-permute-start | bytes 384008 | tf_op jit(solution)/shard_map/ppermute | solution.py:179

commit v6 on v5

--- a/solution.py
+++ b/solution.py
@@ -169,8 +169,10 @@
     tile = kernel_tile(mine, other, center_feats, center_norms, mine_norms)
     pred_mine, pred_other = predictions(tile, coeffs.T)
     land_tile = land_rows(tile, lax.rem(landmark_index, slab))
-    pair = pred_mine + lax.ppermute(pred_other, "centers", swap)
-    sent = (pair * SENT_SCALE).astype(jnp.float16)
+    crossed = lax.ppermute(
+        (pred_other * SENT_SCALE).astype(jnp.float16), "centers", swap
+    )
+    sent = (pred_mine * SENT_SCALE + crossed.astype(jnp.float32)).astype(jnp.float16)
     parts = exchange(sent.reshape(chips, picks, -1)).astype(jnp.float32)
     new_running = running + jnp.sum(parts, axis=0) / SENT_SCALE
     resid = (new_running - labels.astype(jnp.float32)).astype(jnp.bfloat16)

time: 44.6 us -> 44.5 us (level)
  no operation moved by 1% of the time
where the time goes in v6:
time: 44.5 us; the launch traced here: 44.2 us
  blocking collectives  33 us (74%)
  Pallas kernels  3 us (7%)
  waiting for transfers between devices  2.31 us (5%)
  local copies, waits for them, and re-layouts  2.01 us (5%)
  starting transfers between devices  1.29 us (3%)
  matrix products  1.14 us (3%)
  other arithmetic  0.73 us (2%)
  between operations  0.72 us (2%)
    all_to_all x3, blocking collectives, exchange(): lax.all_to_all(blocks, 'centers', 0, 0, axis_index_groups=across, tiled=T...  33 us
    unnamed x12, local copies, waits for them, and re-layouts  1.89 us
    ppermute x1, waiting for transfers between devices, per_device(): lax.ppermute((pred_other * SENT_SCALE).astype(jnp.float16), 'centers', swap)  1.25 us
    dot_general x1, matrix products, per_device(): jnp.dot(land_tile, jnp.concatenate([resid_mine, resid_other], axis=0), pr...  1.14 us
  transfers between devices with their start and end apart: 3, of which 3 were waited for; matrix products, arithmetic and copies ran while one was open for 0% of the time, Pallas kernels for 2%

profile of v6, /device:TPU:0, one launch (start us, length us, event | category | flops | bytes accessed | tf_op | source)
XLA Modules:
  0.0 44.2 jit_solution(8425822365359385534)
XLA Ops:
  0.6 0.0 copy-start
  0.6 0.0 copy-start.2
  0.6 0.8 %copy-done.2 = s32[8]{0:T(128)S(1)} copy-done((s32[8]{0:T(128)S(1)}, s32[8]{0:T(128)}, u32[]{:S(2)}) %copy-start.2) | copy-done | bytes 56
  1.5 0.8 %copy-done = bf16[1024,1024]{1,0:T(8,128)(2,1)S(1)} copy-done((bf16[1024,1024]{1,0:T(8,128)(2,1)S(1)}, bf16[1024,1024]{1,0:T(8,128)(2,1)}, u32[]{:S(2)}) %copy-start) | copy-done | bytes 2097176
  2.2 0.7 %shard_map.78 = bf16[8,8,1024]{2,1,0:T(8,128)(2,1)S(1)} custom-call(s32[8]{0:T(128)S(1)} %shard_map.77.index_ref, bf16[1024,1024]{1,0:T(8,128)(2,1)S(1)} %copy-done), custom_call_target="tpu_custom_call" | custom-call | tf_op jit(solution)/shard_map/pallas_call | solution.py:51
  2.9 13.5 %all_to_all.15 = bf16[8,8,1024]{2,1,0:T(8,128)(2,1)S(1)} all-to-all(bf16[8,8,1024]{2,1,0:T(8,128)(2,1)S(1)} %shard_map.78), channel_id=1, replica_groups={{0,3,5,6,9,10,12,15},{1,2,4,7,8,11,13,14},{16,19,21,22,25,26,28,31},{17..., dimensions={0} | all-to-all | bytes 262144 | tf_op jit(solution)/shard_map/all_to_all | solution.py:159
  16.4 0.7 %collective-permute-start = (bf16[64,1024]{1,0:T(8,128)(2,1)S(1)}, bf16[64,1024]{1,0:T(8,128)(2,1)S(1)}, u32[]{:S(2)}, u32[]{:S(2)}) collective-permute-start(bf16[64,1024]{1,0:T(8,128)(2,1)S(1)} %bitcast.9), channel_id=1, source_target_pairs={{0,1},{1,0},{2,3},{3,2},{4,5},{5,4},{6,7},{7,6},{8,9},{9,8},{10,11... | collective-permute-start | bytes 393224 | tf_op jit(solution)/shard_map/ppermute | solution.py:167
  17.1 0.5 %shard_map.79 = (f32[1024,1]{1,0:T(8,128)S(1)}, f32[64,1]{1,0:T(8,128)S(1)}) custom-call(bf16[64,1024]{1,0:T(8,128)(2,1)S(1)} %bitcast.10, bf16[1024,1024]{1,0:T(8,128)(2,1)S(1)} %copy-done), custom_call_target="tpu_custom_call" | custom-call | tf_op jit(solution)/shard_map/pallas_call | solution.py:76
  17.6 0.0 copy-start.1
  17.6 0.5 %collective-permute-done.other_ref = bf16[64,1024]{1,0:T(8,128)(2,1)S(1)} collective-permute-done((bf16[64,1024]{1,0:T(8,128)(2,1)S(1)}, bf16[64,1024]{1,0:T(8,128)(2,1)S(1)}, u32[]{:S(2)}, u32[]{:S(2)}) %collective-permute-start) | collective-permute-done | bytes 131104 | tf_op jit(solution)/shard_map/ppermute | solution.py:167
  18.1 0.8 %shard_map.80.tile_ref = bf16[1024,128]{1,0:T(8,128)(2,1)S(1)} custom-call(bf16[64,1024]{1,0:T(8,128)(2,1)S(1)} %bitcast.11, bf16[64,1024]{1,0:T(8,128)(2,1)S(1)} %collective-permute-done.other_ref, bf16[1024,1024]{1,0:T(8,128)(2,1)S(1)} %copy-done, f32[1024,1]{1,0:T(8,128)S(1)} %get-tuple-element.6.centers_ref, f32[64,1]{1,0:T(8,128)S(1)} %get-tuple-element.7.mine_norms_ref), custom_call_target="tpu_custom_call" | custom-call | tf_op jit(solution)/shard_map/pallas_call | solution.py:101
  18.8 0.0 copy-start.3
  18.9 0.0 copy-start.4
  18.9 0.3 copy-done.1
  19.2 0.0 copy-start.5
  19.2 0.8 %shard_map.81 = (f32[64,1000]{1,0:T(8,128)S(1)}, f32[64,1000]{1,0:T(8,128)S(1)}) custom-call(bf16[1024,128]{1,0:T(8,128)(2,1)S(1)} %shard_map.80.tile_ref, bf16[1000,1024]{1,0:T(8,128)(2,1)S(1)} %bitcast.8), custom_call_target="tpu_custom_call" | custom-call | tf_op jit(solution)/shard_map/pallas_call | solution.py:144
  20.0 0.2 collective-permute-start.1
  20.1 1.3 %collective-permute-done.1 = f16[64,1000]{1,0:T(8,128)(2,1)S(1)} collective-permute-done((f16[64,1000]{1,0:T(8,128)(2,1)S(1)}, f16[64,1000]{1,0:T(8,128)(2,1)S(1)}, u32[]{:S(2)}, u32[]{:S(2)}) %collective-permute-start.1) | collective-permute-done | bytes 128032 | tf_op jit(solution)/shard_map/ppermute | solution.py:172
  21.4 9.9 %all_to_all.16 = f16[8,8,1000]{2,1,0:T(8,128)(2,1)S(1)} all-to-all(f16[8,8,1000]{2,1,0:T(8,128)(2,1)S(1)} %fusion.4), channel_id=1, replica_groups={{0,3,5,6,9,10,12,15},{1,2,4,7,8,11,13,14},{16,19,21,22,25,26,28,31},{17..., dimensions={0} | all-to-all | bytes 256000 | tf_op jit(solution)/shard_map/all_to_all | solution.py:159
  31.4 0.0 copy-done.3
  31.4 0.0 copy-done.4
  31.4 0.6 %subtract_convert_fusion = (bf16[8,1000]{1,0:T(8,128)(2,1)S(1)}, f32[8,1000]{1,0:T(8,128)}) fusion(bf16[8,1000]{1,0:T(8,128)(2,1)S(1)} %copy-done.4, f32[8,1000]{1,0:T(8,128)S(1)} %copy-done.3, f32[8,1000]{1,0:T(8,128)S(1)} %convert_reduce_fusion), kind=kLoop, calls=%fused_computation.8 | loop fusion | flops 40000 | bytes 128000 | tf_op jit(solution)/shard_map/convert_element_type | solution.py:178
  32.0 9.6 %all_to_all.17 = bf16[8,8,1000]{2,1,0:T(8,128)(2,1)S(1)} all-to-all(bf16[8,8,1000]{2,1,0:T(8,128)(2,1)S(1)} %broadcast_in_dim.3), channel_id=1, replica_groups={{0,3,5,6,9,10,12,15},{1,2,4,7,8,11,13,14},{16,19,21,22,25,26,28,31},{17..., dimensions={0} | all-to-all | bytes 256000 | tf_op jit(solution)/shard_map/all_to_all | solution.py:159
  41.6 0.5 %collective-permute-start.2 = (bf16[64,1000]{1,0:T(8,128)(2,1)S(1)}, bf16[64,1000]{1,0:T(8,128)(2,1)S(1)}, u32[]{:S(2)}, u32[]{:S(2)}) collective-permute-start(bf16[64,1000]{1,0:T(8,128)(2,1)S(1)} %bitcast.12), channel_id=1, source_target_pairs={{0,1},{1,0},{2,3},{3,2},{4,5},{5,4},{6,7},{7,6},{8,9},{9,8},{10,11... | collective-permute-start | bytes 384008 | tf_op jit(solution)/shard_map/ppermute | solution.py:181
  42.1 0.0 copy-done.5
  42.1 0.1 copy.8.land_ref
  42.2 0.3 shard_map.82
  42.5 0.6 %collective-permute-done.2 = bf16[64,1000]{1,0:T(8,128)(2,1)S(1)} collective-permute-done((bf16[64,1000]{1,0:T(8,128)(2,1)S(1)}, bf16[64,1000]{1,0:T(8,128)(2,1)S(1)}, u32[]{:S(2)}, u32[]{:S(2)}) %collective-permute-start.2) | collective-permute-done | bytes 128032 | tf_op jit(solution)/shard_map/ppermute | solution.py:181
  43.1 1.1 %fusion = f32[128,1000]{0,1:T(8,128)} fusion(bf16[128,128]{1,0:T(8,128)(2,1)S(1)} %shard_map.82, bf16[64,1000]{1,0:T(8,128)(2,1)S(1)} %collective-permute-done.2, bf16[64,1000]{1,0:T(8,128)(2,1)S(1)} %bitcast.13), kind=kOutput, calls=%fused_computation | convolution fusion | flops 33280000 | bytes 800768 | tf_op jit(solution)/shard_map/dot_general | solution.py:182
  (6 shorter events, 0.1 us)
Async XLA Ops:
  0.6 1.6 %copy-start = (bf16[1024,1024]{1,0:T(8,128)(2,1)S(1)}, bf16[1024,1024]{1,0:T(8,128)(2,1)}, u32[]{:S(2)}) copy-start(bf16[1024,1024]{1,0:T(8,128)(2,1)} %feats_ref.5) | copy-start | bytes 6291460
  0.6 0.8 %copy-start.2 = (s32[8]{0:T(128)S(1)}, s32[8]{0:T(128)}, u32[]{:S(2)}) copy-start(s32[8]{0:T(128)} %index_ref.1) | copy-start | bytes 100
  16.4 1.7 %collective-permute-start = (bf16[64,1024]{1,0:T(8,128)(2,1)S(1)}, bf16[64,1024]{1,0:T(8,128)(2,1)S(1)}, u32[]{:S(2)}, u32[]{:S(2)}) collective-permute-start(bf16[64,1024]{1,0:T(8,128)(2,1)S(1)} %bitcast.9), channel_id=1, source_target_pairs={{0,1},{1,0},{2,3},{3,2},{4,5},{5,4},{6,7},{7,6},{8,9},{9,8},{10,11... | collective-permute-start | bytes 393224 | tf_op jit(solution)/shard_map/ppermute | solution.py:167
  17.6 1.6 %copy-start.1 = (bf16[1024,1000]{0,1:T(8,128)(2,1)S(1)}, bf16[1024,1000]{0,1:T(8,128)(2,1)}, u32[]{:S(2)}) copy-start(bf16[1024,1000]{0,1:T(8,128)(2,1)} %param.7) | copy-start | bytes 6144004
  18.8 12.5 %copy-start.3 = (f32[8,1000]{1,0:T(8,128)S(1)}, f32[8,1000]{1,0:T(8,128)}, u32[]{:S(2)}) copy-start(f32[8,1000]{1,0:T(8,128)} %param.9) | copy-start | bytes 96004
  18.9 12.5 %copy-start.4 = (bf16[8,1000]{1,0:T(8,128)(2,1)S(1)}, bf16[8,1000]{1,0:T(8,128)(2,1)}, u32[]{:S(2)}) copy-start(bf16[8,1000]{1,0:T(8,128)(2,1)} %param.8) | copy-start | bytes 48004
  19.2 22.9 %copy-start.5 = (s32[128]{0:T(128)S(1)}, s32[128]{0:T(128)}, u32[]{:S(2)}) copy-start(s32[128]{0:T(128)} %param.11) | copy-start | bytes 1540
  20.0 1.4 %collective-permute-start.1 = (f16[64,1000]{1,0:T(8,128)(2,1)S(1)}, f16[64,1000]{1,0:T(8,128)(2,1)S(1)}, u32[]{:S(2)}, u32[]{:S(2)}) collective-permute-start(f16[64,1000]{1,0:T(8,128)(2,1)S(1)} %multiply_convert_fusion), channel_id=1, source_target_pairs={{0,1},{1,0},{2,3},{3,2},{4,5},{5,4},{6,7},{7,6},{8,9},{9,8},{10,11... | collective-permute-start | bytes 384008 | tf_op jit(solution)/shard_map/ppermute | solution.py:172
  41.6 1.4 %collective-permute-start.2 = (bf16[64,1000]{1,0:T(8,128)(2,1)S(1)}, bf16[64,1000]{1,0:T(8,128)(2,1)S(1)}, u32[]{:S(2)}, u32[]{:S(2)}) collective-permute-start(bf16[64,1000]{1,0:T(8,128)(2,1)S(1)} %bitcast.12), channel_id=1, source_target_pairs={{0,1},{1,0},{2,3},{3,2},{4,5},{5,4},{6,7},{7,6},{8,9},{9,8},{10,11... | collective-permute-start | bytes 384008 | tf_op jit(solution)/shard_map/ppermute | solution.py:181

commit v7 on v6

--- a/solution.py
+++ b/solution.py
@@ -173,11 +173,19 @@
         (pred_other * SENT_SCALE).astype(jnp.float16), "centers", swap
     )
     sent = (pred_mine * SENT_SCALE + crossed.astype(jnp.float32)).astype(jnp.float16)
-    parts = exchange(sent.reshape(chips, picks, -1)).astype(jnp.float32)
-    new_running = running + jnp.sum(parts, axis=0) / SENT_SCALE
-    resid = (new_running - labels.astype(jnp.float32)).astype(jnp.bfloat16)
+    parts = exchange(sent.reshape(chips, picks, -1))
+
+    def updated(running, parts):
+        return running + jnp.sum(parts.astype(jnp.float32), axis=0) / SENT_SCALE
+
+    resid = updated(running, parts) - labels.astype(jnp.float32)
+    resid = resid.astype(jnp.bfloat16)
     resid = jnp.broadcast_to(resid, (chips,) + resid.shape)
     resid_mine = exchange(resid).reshape(chips * picks, -1)
+    later_running, later_parts, resid_mine = lax.optimization_barrier(
+        (running, parts, resid_mine)
+    )
+    new_running = updated(later_running, later_parts)
     resid_other = lax.ppermute(resid_mine, "centers", swap)
     projection = jnp.dot(
         land_tile,

time: 44.5 us -> 45.5 us (1.022)
  blocking collectives: 33 us -> 23.4 us
  waiting for transfers between devices: 2.31 us -> 8.78 us
  starting transfers between devices: 1.29 us -> 4.66 us
  local copies, waits for them, and re-layouts: 2.01 us -> 2.65 us
    all_to_all x3 -> x2, blocking collectives: 33 us -> 23.4 us  [exchange(): lax.all_to_all(blocks, 'centers', 0, 0, axis_index_groups=across, tiled=T...]
    all_to_all x0 -> x1, waiting for transfers between devices: none -> 6.7 us  [exchange(): lax.all_to_all(blocks, 'centers', 0, 0, axis_index_groups=across, tiled=T...]
    all_to_all x0 -> x1, starting transfers between devices: none -> 3.37 us  [exchange(): lax.all_to_all(blocks, 'centers', 0, 0, axis_index_groups=across, tiled=T...]
    broadcast_in_dim x1, local copies, waits for them, and re-layouts: 0.01 us -> 0.66 us  [per_device(): resid = jnp.broadcast_to(resid, (chips,) + resid.shape)]
    add x0 -> x1, other arithmetic: none -> 0.62 us  [updated(): return running + jnp.sum(parts.astype(jnp.float32), axis=0) / SENT_SCALE]
    convert_element_type x1, other arithmetic: 0.62 us -> 0.01 us  [per_device(): resid = resid.astype(jnp.bfloat16)]
  transfers between devices with their start and end apart: 3 -> 4, of which waited for: 3 -> 4; matrix products, arithmetic and copies ran while one was open for 0% -> 2% of each run, Pallas kernels for 2% -> 2%
where the time goes in v7:
time: 45.5 us; the launch traced here: 45.2 us
  blocking collectives  23.4 us (51%)
  waiting for transfers between devices  8.78 us (19%)
  starting transfers between devices  4.66 us (10%)
  Pallas kernels  3 us (7%)
  local copies, waits for them, and re-layouts  2.65 us (6%)
  matrix products  1.14 us (3%)
  other arithmetic  0.76 us (2%)
  between operations  0.75 us (2%)
    all_to_all x2, blocking collectives, exchange(): lax.all_to_all(blocks, 'centers', 0, 0, axis_index_groups=across, tiled=T...  23.4 us
    all_to_all x1, waiting for transfers between devices, exchange(): lax.all_to_all(blocks, 'centers', 0, 0, axis_index_groups=across, tiled=T...  6.7 us
    all_to_all x1, starting transfers between devices, exchange(): lax.all_to_all(blocks, 'centers', 0, 0, axis_index_groups=across, tiled=T...  3.37 us
    unnamed x12, local copies, waits for them, and re-layouts  1.88 us
    ppermute x1, waiting for transfers between devices, per_device(): lax.ppermute((pred_other * SENT_SCALE).astype(jnp.float16), 'centers', swap)  1.25 us
    dot_general x1, matrix products, per_device(): jnp.dot(land_tile, jnp.concatenate([resid_mine, resid_other], axis=0), pr...  1.14 us
  transfers between devices with their start and end apart: 4, of which 4 were waited for; matrix products, arithmetic and copies ran while one was open for 2% of the time, Pallas kernels for 2%

profile of v7, /device:TPU:0, one launch (start us, length us, event | category | flops | bytes accessed | tf_op | source)
XLA Modules:
  0.0 45.2 jit_solution(15365686428373115274)
XLA Ops:
  0.6 0.0 copy-start
  0.6 0.0 copy-start.2
  0.6 0.8 %copy-done.2 = s32[8]{0:T(128)S(1)} copy-done((s32[8]{0:T(128)S(1)}, s32[8]{0:T(128)}, u32[]{:S(2)}) %copy-start.2) | copy-done | bytes 56
  1.5 0.8 %copy-done = bf16[1024,1024]{1,0:T(8,128)(2,1)S(1)} copy-done((bf16[1024,1024]{1,0:T(8,128)(2,1)S(1)}, bf16[1024,1024]{1,0:T(8,128)(2,1)}, u32[]{:S(2)}) %copy-start) | copy-done | bytes 2097176
  2.2 0.7 %shard_map.78 = bf16[8,8,1024]{2,1,0:T(8,128)(2,1)S(1)} custom-call(s32[8]{0:T(128)S(1)} %shard_map.77.index_ref, bf16[1024,1024]{1,0:T(8,128)(2,1)S(1)} %copy-done), custom_call_target="tpu_custom_call" | custom-call | tf_op jit(solution)/shard_map/pallas_call | solution.py:51
  2.9 13.5 %all_to_all.15 = bf16[8,8,1024]{2,1,0:T(8,128)(2,1)S(1)} all-to-all(bf16[8,8,1024]{2,1,0:T(8,128)(2,1)S(1)} %shard_map.78), channel_id=1, replica_groups={{0,3,5,6,9,10,12,15},{1,2,4,7,8,11,13,14},{16,19,21,22,25,26,28,31},{17..., dimensions={0} | all-to-all | bytes 262144 | tf_op jit(solution)/shard_map/all_to_all | solution.py:159
  16.4 0.7 %collective-permute-start = (bf16[64,1024]{1,0:T(8,128)(2,1)S(1)}, bf16[64,1024]{1,0:T(8,128)(2,1)S(1)}, u32[]{:S(2)}, u32[]{:S(2)}) collective-permute-start(bf16[64,1024]{1,0:T(8,128)(2,1)S(1)} %bitcast.9), channel_id=1, source_target_pairs={{0,1},{1,0},{2,3},{3,2},{4,5},{5,4},{6,7},{7,6},{8,9},{9,8},{10,11... | collective-permute-start | bytes 393224 | tf_op jit(solution)/shard_map/ppermute | solution.py:167
  17.1 0.5 %shard_map.79 = (f32[1024,1]{1,0:T(8,128)S(1)}, f32[64,1]{1,0:T(8,128)S(1)}) custom-call(bf16[64,1024]{1,0:T(8,128)(2,1)S(1)} %bitcast.10, bf16[1024,1024]{1,0:T(8,128)(2,1)S(1)} %copy-done), custom_call_target="tpu_custom_call" | custom-call | tf_op jit(solution)/shard_map/pallas_call | solution.py:76
  17.6 0.0 copy-start.1
  17.6 0.5 %collective-permute-done.other_ref = bf16[64,1024]{1,0:T(8,128)(2,1)S(1)} collective-permute-done((bf16[64,1024]{1,0:T(8,128)(2,1)S(1)}, bf16[64,1024]{1,0:T(8,128)(2,1)S(1)}, u32[]{:S(2)}, u32[]{:S(2)}) %collective-permute-start) | collective-permute-done | bytes 131104 | tf_op jit(solution)/shard_map/ppermute | solution.py:167
  18.1 0.8 %shard_map.80.tile_ref = bf16[1024,128]{1,0:T(8,128)(2,1)S(1)} custom-call(bf16[64,1024]{1,0:T(8,128)(2,1)S(1)} %bitcast.11, bf16[64,1024]{1,0:T(8,128)(2,1)S(1)} %collective-permute-done.other_ref, bf16[1024,1024]{1,0:T(8,128)(2,1)S(1)} %copy-done, f32[1024,1]{1,0:T(8,128)S(1)} %get-tuple-element.9.centers_ref, f32[64,1]{1,0:T(8,128)S(1)} %get-tuple-element.10.mine_norms_ref), custom_call_target="tpu_custom_call" | custom-call | tf_op jit(solution)/shard_map/pallas_call | solution.py:101
  18.8 0.0 copy-start.3
  18.9 0.0 copy-start.4
  18.9 0.0 copy-start.5
  18.9 0.3 copy-done.1
  19.2 0.8 %shard_map.81 = (f32[64,1000]{1,0:T(8,128)S(1)}, f32[64,1000]{1,0:T(8,128)S(1)}) custom-call(bf16[1024,128]{1,0:T(8,128)(2,1)S(1)} %shard_map.80.tile_ref, bf16[1000,1024]{1,0:T(8,128)(2,1)S(1)} %bitcast.8), custom_call_target="tpu_custom_call" | custom-call | tf_op jit(solution)/shard_map/pallas_call | solution.py:144
  20.0 0.2 collective-permute-start.1
  20.1 1.2 %collective-permute-done.1 = f16[64,1000]{1,0:T(8,128)(2,1)S(1)} collective-permute-done((f16[64,1000]{1,0:T(8,128)(2,1)S(1)}, f16[64,1000]{1,0:T(8,128)(2,1)S(1)}, u32[]{:S(2)}, u32[]{:S(2)}) %collective-permute-start.1) | collective-permute-done | bytes 128032 | tf_op jit(solution)/shard_map/ppermute | solution.py:172
  21.4 9.9 %all_to_all.16 = f16[8,8,1000]{2,1,0:T(8,128)(2,1)S(1)} all-to-all(f16[8,8,1000]{2,1,0:T(8,128)(2,1)S(1)} %fusion.4), channel_id=1, replica_groups={{0,3,5,6,9,10,12,15},{1,2,4,7,8,11,13,14},{16,19,21,22,25,26,28,31},{17..., dimensions={0} | all-to-all | bytes 256000 | tf_op jit(solution)/shard_map/all_to_all | solution.py:159
  31.4 0.0 copy-done.3
  31.4 0.0 copy-done.4
  31.4 0.7 %broadcast_in_dim.3 = bf16[8,8,1000]{2,1,0:T(8,128)(2,1)} broadcast(bf16[8,1000]{1,0:T(8,128)(2,1)S(1)} %subtract_convert_fusion), dimensions={1,2} | broadcast | bytes 144000 | tf_op jit(solution)/shard_map/broadcast_in_dim | solution.py:183
  32.1 3.4 %all-to-all-start.2 = ((bf16[8,8,1000]{2,1,0:T(8,128)(2,1)}), bf16[8,8,1000]{2,1,0:T(8,128)(2,1)S(1)}, u32[]{:S(2)}, u32[]{:S(2)}) async-start(bf16[8,8,1000]{2,1,0:T(8,128)(2,1)} %broadcast_in_dim.3), calls=%async_computation.2 | async-start | bytes 262144 | tf_op jit(solution)/shard_map/all_to_all | solution.py:159
  35.5 0.0 copy-done.5
  35.5 0.1 copy.8.land_ref
  35.6 0.3 shard_map.82
  35.9 6.7 %all-to-all-done.2 = bf16[8,8,1000]{2,1,0:T(8,128)(2,1)S(1)} async-done(((bf16[8,8,1000]{2,1,0:T(8,128)(2,1)}), bf16[8,8,1000]{2,1,0:T(8,128)(2,1)S(1)}, u32[]{:S(2)}, u32[]{:S(2)}) %all-to-all-start.2) | async-done | bytes 128032 | tf_op jit(solution)/shard_map/all_to_all | solution.py:159
  42.6 0.5 collective-permute-start.2
  43.1 0.6 %multiply_add_fusion = f32[8,1000]{1,0:T(8,128)} fusion(f32[8,1000]{1,0:T(8,128)S(1)} %copy-done.3, f32[8,1000]{1,0:T(8,128)S(1)} %convert_reduce_fusion), kind=kLoop, calls=%fused_computation.9 | loop fusion | flops 16000 | bytes 96000 | tf_op jit(solution)/shard_map/add | solution.py:179
  43.7 0.3 collective-permute-done.2
  44.0 1.1 %fusion = f32[128,1000]{0,1:T(8,128)} fusion(bf16[128,128]{1,0:T(8,128)(2,1)S(1)} %shard_map.82, bf16[64,1000]{1,0:T(8,128)(2,1)S(1)} %collective-permute-done.2, bf16[64,1000]{1,0:T(8,128)(2,1)S(1)} %bitcast.13), kind=kOutput, calls=%fused_computation | convolution fusion | flops 33280000 | bytes 800768 | tf_op jit(solution)/shard_map/dot_general | solution.py:190
  (7 shorter events, 0.1 us)
Async XLA Ops:
  0.6 1.6 %copy-start = (bf16[1024,1024]{1,0:T(8,128)(2,1)S(1)}, bf16[1024,1024]{1,0:T(8,128)(2,1)}, u32[]{:S(2)}) copy-start(bf16[1024,1024]{1,0:T(8,128)(2,1)} %feats_ref.5) | copy-start | bytes 6291460
  0.6 0.8 %copy-start.2 = (s32[8]{0:T(128)S(1)}, s32[8]{0:T(128)}, u32[]{:S(2)}) copy-start(s32[8]{0:T(128)} %index_ref.1) | copy-start | bytes 100
  16.4 1.7 %collective-permute-start = (bf16[64,1024]{1,0:T(8,128)(2,1)S(1)}, bf16[64,1024]{1,0:T(8,128)(2,1)S(1)}, u32[]{:S(2)}, u32[]{:S(2)}) collective-permute-start(bf16[64,1024]{1,0:T(8,128)(2,1)S(1)} %bitcast.9), channel_id=1, source_target_pairs={{0,1},{1,0},{2,3},{3,2},{4,5},{5,4},{6,7},{7,6},{8,9},{9,8},{10,11... | collective-permute-start | bytes 393224 | tf_op jit(solution)/shard_map/ppermute | solution.py:167
  17.6 1.6 %copy-start.1 = (bf16[1024,1000]{0,1:T(8,128)(2,1)S(1)}, bf16[1024,1000]{0,1:T(8,128)(2,1)}, u32[]{:S(2)}) copy-start(bf16[1024,1000]{0,1:T(8,128)(2,1)} %param.7) | copy-start | bytes 6144004
  18.8 12.5 %copy-start.3 = (f32[8,1000]{1,0:T(8,128)S(1)}, f32[8,1000]{1,0:T(8,128)}, u32[]{:S(2)}) copy-start(f32[8,1000]{1,0:T(8,128)} %param.9) | copy-start | bytes 96004
  18.9 12.5 %copy-start.4 = (bf16[8,1000]{1,0:T(8,128)(2,1)S(1)}, bf16[8,1000]{1,0:T(8,128)(2,1)}, u32[]{:S(2)}) copy-start(bf16[8,1000]{1,0:T(8,128)(2,1)} %param.8) | copy-start | bytes 48004
  18.9 16.6 %copy-start.5 = (s32[128]{0:T(128)S(1)}, s32[128]{0:T(128)}, u32[]{:S(2)}) copy-start(s32[128]{0:T(128)} %param.11) | copy-start | bytes 1540
  20.0 1.4 %collective-permute-start.1 = (f16[64,1000]{1,0:T(8,128)(2,1)S(1)}, f16[64,1000]{1,0:T(8,128)(2,1)S(1)}, u32[]{:S(2)}, u32[]{:S(2)}) collective-permute-start(f16[64,1000]{1,0:T(8,128)(2,1)S(1)} %multiply_convert_fusion), channel_id=1, source_target_pairs={{0,1},{1,0},{2,3},{3,2},{4,5},{5,4},{6,7},{7,6},{8,9},{9,8},{10,11... | collective-permute-start | bytes 384008 | tf_op jit(solution)/shard_map/ppermute | solution.py:172
  32.1 10.5 %all-to-all-start.2 = ((bf16[8,8,1000]{2,1,0:T(8,128)(2,1)}), bf16[8,8,1000]{2,1,0:T(8,128)(2,1)S(1)}, u32[]{:S(2)}, u32[]{:S(2)}) async-start(bf16[8,8,1000]{2,1,0:T(8,128)(2,1)} %broadcast_in_dim.3), calls=%async_computation.2 | async-start | bytes 262144 | tf_op jit(solution)/shard_map/all_to_all | solution.py:159
  42.6 1.4 %collective-permute-start.2 = (bf16[64,1000]{1,0:T(8,128)(2,1)S(1)}, bf16[64,1000]{1,0:T(8,128)(2,1)S(1)}, u32[]{:S(2)}, u32[]{:S(2)}) collective-permute-start(bf16[64,1000]{1,0:T(8,128)(2,1)S(1)} %bitcast.12), channel_id=1, source_target_pairs={{0,1},{1,0},{2,3},{3,2},{4,5},{5,4},{6,7},{7,6},{8,9},{9,8},{10,11... | collective-permute-start | bytes 384008 | tf_op jit(solution)/shard_map/ppermute | solution.py:189
